TPU v7x, 512 devices: a whole 4x8x8 slice. The times are simulated.
512 devices in a mesh: segment: 4 (over x_hi, core), lat: 128 (over z, y, x_lo).
Axes of the slice: x: 4 (x_hi: 2, x_lo: 2; x = x_hi * 2 + x_lo), y: 8, z: 8, core: 2. Of those that a mesh axis runs over, the one named last changes fastest.
Arguments:
- fields: bfloat16 [4, 21504, 144], P('segment', 'lat'), may hold values from -6 to 6
- band_rows: int32 [128], replicated, may hold values from 1 to 2, 192 in all
- window_table: int32 [128], replicated, may hold values from -1 to 118, as said below
- level_embed: bfloat16 [2, 1024], replicated, may hold values from -6 to 6
- embed_weight: bfloat16 [144, 1024], replicated, may hold values from -0.5 to 0.5
- attn_weight: bfloat16 [4, 1024, 4096], P('segment', None, 'lat'), may hold values from -0.1875 to 0.1875
- norm_gain: float32 [4, 1024], P('segment'), may hold values from 0.5 to 1.5
- head_weight: bfloat16 [1024, 144], replicated, may hold values from -0.1875 to 0.1875
Outputs:
- decoded: bfloat16 [4, 21504, 144], P('segment', 'lat')
- window_decoded: bfloat16 [4, 18432, 144], P('segment', 'lat')
Inputs may be any that keep to these rules, and one draw needn't show every extreme that they name: `window_table`: each window 0 to 118 appears once, other shards hold -1. `band_rows`: rows of each band sum to 192.
All inputs are finite; a program needn't handle non-finite values.
Results may differ from a plain program's by a relative error of at most 0.025.
Values may be sent and summed in bfloat16 or wider, within the bound.
No kernel may reach another device: no remote copies, remote signals or barrier semaphores. Data moves between devices by JAX's collectives and lax.ppermute only.
A program may use at most 64 MiB of HBM per device.

v0:
```python
import math

import jax
import jax.numpy as jnp
from jax import lax
from jax.sharding import PartitionSpec as P

HEAD_DIM = 64
LEV = 2
WIN_ROWS = 12
WIN_COLS = 6
WTOK = 144
CAP = 24


def shifted(value, axis, by):
    count = lax.axis_size(axis)
    pairs = [(i, i + by) for i in range(count) if 0 <= i + by < count]
    return lax.ppermute(value, axis, pairs)


def from_root(value, axis, root):
    mine = lax.axis_index(axis) == root
    return lax.psum(jnp.where(mine, value, jnp.zeros_like(value)), axis)


def attend_block(tokens, gain, weight, allowed):
    width = tokens.shape[-1]
    heads = width // HEAD_DIM
    wide = tokens.astype(jnp.float32)
    normed = (
        wide * lax.rsqrt(jnp.mean(wide * wide, axis=-1, keepdims=True) + 1e-06) * gain
    ).astype(jnp.bfloat16)
    project = jnp.dot(normed, weight[:, : 3 * width], preferred_element_type=jnp.float32).astype(
        jnp.bfloat16
    )
    query = project[:, :width].reshape(-1, heads, HEAD_DIM)
    keyed = project[:, width : 2 * width].reshape(-1, heads, HEAD_DIM)
    valued = project[:, 2 * width :].reshape(-1, heads, HEAD_DIM)
    scores = jnp.einsum(
        "qhd,khd->hqk", query, keyed, preferred_element_type=jnp.float32
    ) / math.sqrt(HEAD_DIM)
    scores = jnp.where(allowed[None], scores, -1e30)
    probs = jax.nn.softmax(scores, axis=-1).astype(jnp.bfloat16)
    mixed = (
        jnp.einsum("hqk,khd->qhd", probs, valued, preferred_element_type=jnp.float32)
        .astype(jnp.bfloat16)
        .reshape(-1, width)
    )
    update = jnp.dot(mixed, weight[:, 3 * width :], preferred_element_type=jnp.float32)
    return (wide + update).astype(jnp.bfloat16)


def per_device(
    fields, band_rows, window_table, level_embed, embed_weight, attn_weight, norm_gain, head_weight
):
    lat_count = lax.axis_size("lat")
    segment_count = lax.axis_size("segment")
    lat_index = lax.axis_index("lat")
    segment_index = lax.axis_index("segment")
    slab_dev = fields.shape[0]
    slab_total = slab_dev * segment_count
    total_rows = 3 * lat_count // 2
    lon_windows = lat_count // (lat_count // 8 + 1)
    lon_cells = WIN_COLS * lon_windows
    row_ends = jnp.cumsum(band_rows)
    row_starts = row_ends - band_rows
    my_start = row_starts[lat_index]
    my_rows = band_rows[lat_index]
    slot = jnp.arange(CAP, dtype=jnp.int32)
    slot_row = slot // (WIN_COLS * LEV)
    slot_col = slot // LEV % WIN_COLS
    slot_lev = slot % LEV
    target = window_table[:, None]
    target_first = WIN_ROWS * (target // lon_windows) - WIN_ROWS // 2
    send_grid = my_start + slot_row[None]
    usable = (
        (target >= 0)
        & (slot_row[None] < my_rows)
        & (send_grid >= target_first)
        & (send_grid < target_first + WIN_ROWS)
    )
    band_slot = (
        slot_row[None] * lon_cells + WIN_COLS * (target % lon_windows) + slot_col[None]
    ) * LEV + slot_lev[None]
    band_slot = jnp.where(usable, band_slot, 0)
    outgoing = jnp.take(fields, band_slot.reshape(-1), axis=1).reshape(slab_dev, lat_count, CAP, -1)
    outgoing = outgoing * usable[None, :, :, None].astype(fields.dtype)
    arrived = lax.all_to_all(outgoing, "lat", split_axis=1, concat_axis=1, tiled=True)
    token = jnp.arange(WTOK, dtype=jnp.int32)
    level = token // (WIN_ROWS * WIN_COLS)
    lat_off = token // WIN_COLS % WIN_ROWS
    lon_off = token % WIN_COLS
    my_window = window_table[lat_index]
    first_row = WIN_ROWS * (my_window // lon_windows) - WIN_ROWS // 2
    token_grid = first_row + lat_off
    keep = (my_window >= 0) & (token_grid >= 0) & (token_grid < total_rows)
    band_of = jnp.sum((row_ends[None, :] <= token_grid[:, None]).astype(jnp.int32), axis=-1)
    band_of = jnp.clip(band_of, 0, lat_count - 1)
    local_row = token_grid - row_starts[band_of]
    picks = band_of * CAP + (local_row * WIN_COLS + lon_off) * LEV + level
    picks = jnp.where(keep, picks, 0)
    raw_tokens = jnp.take(arrived.reshape(slab_dev, lat_count * CAP, -1), picks, axis=1)
    raw_tokens = raw_tokens * keep[None, :, None].astype(fields.dtype)
    all_raw = lax.all_gather(raw_tokens, "segment", axis=0, tiled=True)
    weight = lax.all_gather(attn_weight[0], "lat", axis=1, tiled=True)
    gain = norm_gain[0]
    width = embed_weight.shape[1]
    level_rows = jnp.broadcast_to(
        level_embed.astype(jnp.float32)[:, None, :], (LEV, WIN_ROWS * WIN_COLS, width)
    ).reshape(WTOK, width)
    same_column = (lat_off[:, None] == lat_off[None, :]) & (lon_off[:, None] == lon_off[None, :])
    window_keys = jnp.broadcast_to(keep[None, :], (WTOK, WTOK))
    edge_segment = (segment_index == 0) | (segment_index == segment_count - 1)
    allowed = jnp.where(edge_segment, same_column, window_keys)
    keep_wide = keep[:, None].astype(jnp.float32)

    def tick_step(tick, carry):
        buffer, finished = carry
        slab = tick - segment_index
        active = (slab >= 0) & (slab < slab_total)
        slab_at = jnp.clip(slab, 0, slab_total - 1)

        def run_section(operand):
            incoming, done = operand

            def embed_slab():
                current = lax.dynamic_index_in_dim(all_raw, slab_at, 0, keepdims=False)
                return (
                    jnp.dot(current, embed_weight, preferred_element_type=jnp.float32) + level_rows
                ).astype(jnp.bfloat16)

            def pass_along():
                return incoming

            start_tokens = lax.cond(segment_index == 0, embed_slab, pass_along)
            hidden = attend_block(start_tokens, gain, weight, allowed)

            def store_head():
                result = (
                    jnp.dot(hidden, head_weight, preferred_element_type=jnp.float32) * keep_wide
                ).astype(jnp.bfloat16)
                return lax.dynamic_update_index_in_dim(done, result, slab_at, 0)

            def keep_done():
                return done

            done = lax.cond(segment_index == segment_count - 1, store_head, keep_done)
            return (hidden, done)

        def skip_section(operand):
            return operand

        hidden, finished = lax.cond(active, run_section, skip_section, (buffer, finished))
        buffer = shifted(hidden, "segment", 1)
        return (buffer, finished)

    start_buffer = jnp.zeros((WTOK, width), jnp.bfloat16)
    start_done = jnp.zeros((slab_total, WTOK, head_weight.shape[1]), jnp.bfloat16)
    buffer, finished = lax.fori_loop(
        0, slab_total + segment_count - 1, tick_step, (start_buffer, start_done)
    )
    everyone = from_root(finished, "segment", segment_count - 1)
    own_slabs = lax.dynamic_slice_in_dim(everyone, segment_index * slab_dev, slab_dev, 0)
    back_grid = row_starts[:, None] + slot_row[None]
    usable_back = (
        (my_window >= 0)
        & (slot_row[None] < band_rows[:, None])
        & (back_grid >= first_row)
        & (back_grid < first_row + WIN_ROWS)
    )
    token_index = (slot_lev[None] * WIN_ROWS + (back_grid - first_row)) * WIN_COLS + slot_col[None]
    token_index = jnp.where(usable_back, token_index, 0)
    returning = jnp.take(own_slabs, token_index.reshape(-1), axis=1).reshape(
        slab_dev, lat_count, CAP, -1
    )
    returning = returning * usable_back[None, :, :, None].astype(own_slabs.dtype)
    came_back = lax.all_to_all(returning, "lat", split_axis=1, concat_axis=1, tiled=True)
    band_slot_all = jnp.arange(fields.shape[1], dtype=jnp.int32)
    own_row = band_slot_all // (lon_cells * LEV)
    own_col = band_slot_all // LEV % lon_cells
    own_lev = band_slot_all % LEV
    present = own_row < my_rows
    own_grid = my_start + own_row
    window_row = (own_grid + WIN_ROWS // 2) // WIN_ROWS
    window_id = window_row * lon_windows + own_col // WIN_COLS
    shard_ids = jnp.arange(lat_count, dtype=jnp.int32)
    holder = jnp.sum(
        shard_ids[None, :] * (window_table[None, :] == window_id[:, None]).astype(jnp.int32), axis=1
    )
    pick_back = holder * CAP + (own_row * WIN_COLS + own_col % WIN_COLS) * LEV + own_lev
    pick_back = jnp.where(present, pick_back, 0)
    decoded = jnp.take(came_back.reshape(slab_dev, lat_count * CAP, -1), pick_back, axis=1)
    decoded = decoded * present[None, :, None].astype(came_back.dtype)
    return (decoded, own_slabs)


def solution(mesh):
    placed = (
        P("segment", "lat", None),
        P(),
        P(),
        P(),
        P(),
        P("segment", None, "lat"),
        P("segment", None),
        P(),
    )
    return jax.shard_map(
        per_device,
        mesh=mesh,
        in_specs=placed,
        out_specs=(P("segment", "lat", None), P("segment", "lat", None)),
        check_vma=False,
    )
```

profile of v0, /device:TPU:10, one launch (start us, length us, event | category | flops | bytes accessed | tf_op | source)
XLA Modules:
  0.0 909.6 jit_solution(15150056025346222725)
XLA Ops:
  21.0 11.1 %gather_fusion.1 = bf16[3072,144]{1,0:T(8,128)(2,1)S(1)} fusion(bf16[168,144]{1,0:T(8,128)(2,1)S(1)} %bitcast.64, s32[3072]{0:T(1024)S(1)} %broadcast_clamp_fusion.1), kind=kCustom, calls=%fused_computation.1 | custom fusion | bytes 1781760 | tf_op jit(solution)/shard_map/jit(_take)/gather | solution.py:87
  34.4 18.4 %all-to-all-start = ((bf16[1,128,24,144]{3,2,0,1:T(8,128)(2,1)}), bf16[1,128,24,144]{3,2,0,1:T(8,128)(2,1)S(1)}, u32[]{:S(2)}, u32[]{:S(2)}) async-start(bf16[1,128,24,144]{3,2,0,1:T(8,128)(2,1)} %select_multiply_fusion.1), calls=%async_computation | async-start | bytes 3145728 | tf_op jit(solution)/shard_map/all_to_all | solution.py:89
  55.6 44.9 %all-to-all-done = bf16[1,128,24,144]{3,2,0,1:T(8,128)(2,1)S(1)} async-done(((bf16[1,128,24,144]{3,2,0,1:T(8,128)(2,1)}), bf16[1,128,24,144]{3,2,0,1:T(8,128)(2,1)S(1)}, u32[]{:S(2)}, u32[]{:S(2)}) %all-to-all-start) | async-done | bytes 884768 | tf_op jit(solution)/shard_map/all_to_all | solution.py:89
  101.5 8.2 all_gather.6
  109.6 508.6 %all-gather.3.cloned.1.call-done = bf16[1,1024,4096]{1,2,0:T(8,128)(2,1)} async-done(((bf16[1,1024,32]{1,2,0:T(8,128)(2,1)}), bf16[1,1024,4096]{1,2,0:T(8,128)(2,1)}) %all-gather.3.cloned.1.call-update) | async-done | bytes 8388624 | tf_op jit(solution)/shard_map/all_gather | solution.py:106
  618.3 11.4 %copy.61 = bf16[1024,4096]{1,0:T(8,128)(2,1)} copy(bf16[1024,4096]{0,1:T(8,128)(2,1)} %bitcast.69) | data formatting | bytes 16777216
  631.2 136.8 %while.22 = (s32[]{:T(128)}, bf16[144,1024]{1,0:T(8,128)(2,1)}, bf16[4,144,144]{2,1,0:T(8,128)(2,1)}, s32[]{:T(128)}, bf16[4,144,144]{2,1,0:T(8,128)(2,1)}, /*in...) while((s32[]{:T(128)}, bf16[144,1024]{1,0:T(8,128)(2,1)}, ...), condition=%wide.region_14.15_spmd.clone, body=%wide.region_3.14_spmd.clone.sunk | while | flops 1382011520 | bytes 23065500 | solution.py:160
  631.3 13.5 %conditional.5 = ((bf16[144,1024]{1,0:T(8,128)(2,1)}, bf16[4,144,144]{2,1,0:T(8,128)(2,1)})) conditional(s32[]{:T(128)} %convert_element_type.139, (bf16[144,1024]{1,0:T(8,128)(2,1)}, bf16[4,144,144]{2,1,0:T(8,128)(2,1)}) %tuple.93, (s32[]{:T(128)}, s32[]{:T(128)}, bf16[144,1024]{1,0:T(8,128)(2,1)}, bf16[4,144,144]{2,1,0:T(8,128)(2,1)}, ...), branch_computations={%region_4.4_spmd, %region_5.13_spmd} | conditional | flops 1382008576 | bytes 20697030 | solution.py:154
  632.8 3.9 fusion.17
  637.5 2.5 fusion.82
  642.0 2.8 fusion.26
  648.3 13.5 %conditional.5 = ((bf16[144,1024]{1,0:T(8,128)(2,1)}, bf16[4,144,144]{2,1,0:T(8,128)(2,1)})) conditional(s32[]{:T(128)} %convert_element_type.139, (bf16[144,1024]{1,0:T(8,128)(2,1)}, bf16[4,144,144]{2,1,0:T(8,128)(2,1)}) %tuple.93, (s32[]{:T(128)}, s32[]{:T(128)}, bf16[144,1024]{1,0:T(8,128)(2,1)}, bf16[4,144,144]{2,1,0:T(8,128)(2,1)}, ...), branch_computations={%region_4.4_spmd, %region_5.13_spmd} | conditional | flops 1382008576 | bytes 20697030 | solution.py:154
  649.8 3.9 fusion.17
  654.5 2.5 fusion.82
  659.0 2.8 fusion.26
  666.0 13.5 %conditional.5 = ((bf16[144,1024]{1,0:T(8,128)(2,1)}, bf16[4,144,144]{2,1,0:T(8,128)(2,1)})) conditional(s32[]{:T(128)} %convert_element_type.139, (bf16[144,1024]{1,0:T(8,128)(2,1)}, bf16[4,144,144]{2,1,0:T(8,128)(2,1)}) %tuple.93, (s32[]{:T(128)}, s32[]{:T(128)}, bf16[144,1024]{1,0:T(8,128)(2,1)}, bf16[4,144,144]{2,1,0:T(8,128)(2,1)}, ...), branch_computations={%region_4.4_spmd, %region_5.13_spmd} | conditional | flops 1382008576 | bytes 20697030 | solution.py:154
  667.6 3.9 fusion.17
  672.2 2.5 fusion.82
  676.7 2.8 fusion.26
  679.6 4.2 collective-permute-start
  686.0 13.5 %conditional.5 = ((bf16[144,1024]{1,0:T(8,128)(2,1)}, bf16[4,144,144]{2,1,0:T(8,128)(2,1)})) conditional(s32[]{:T(128)} %convert_element_type.139, (bf16[144,1024]{1,0:T(8,128)(2,1)}, bf16[4,144,144]{2,1,0:T(8,128)(2,1)}) %tuple.93, (s32[]{:T(128)}, s32[]{:T(128)}, bf16[144,1024]{1,0:T(8,128)(2,1)}, bf16[4,144,144]{2,1,0:T(8,128)(2,1)}, ...), branch_computations={%region_4.4_spmd, %region_5.13_spmd} | conditional | flops 1382008576 | bytes 20697030 | solution.py:154
  687.6 3.9 fusion.17
  692.2 2.5 fusion.82
  696.7 2.8 fusion.26
  699.5 8.1 collective-permute-start
  709.8 21.6 %collective-permute-start = (bf16[144,1024]{1,0:T(8,128)(2,1)}, bf16[144,1024]{1,0:T(8,128)(2,1)S(1)}, u32[]{:S(2)}, u32[]{:S(2)}) collective-permute-start(bf16[144,1024]{1,0:T(8,128)(2,1)} %get-tuple-element.624), channel_id=1, source_target_pairs={{0,128},{128,256},{256,384},{1,129},{129,257},{257,385},{2,130},{1... | collective-permute-start | bytes 884744 | tf_op jit(solution)/shard_map/while/body/eval_jaxpr/ppermute | solution.py:19
  733.7 8.4 collective-permute-start
  744.2 21.6 %collective-permute-start = (bf16[144,1024]{1,0:T(8,128)(2,1)}, bf16[144,1024]{1,0:T(8,128)(2,1)S(1)}, u32[]{:S(2)}, u32[]{:S(2)}) collective-permute-start(bf16[144,1024]{1,0:T(8,128)(2,1)} %get-tuple-element.624), channel_id=1, source_target_pairs={{0,128},{128,256},{256,384},{1,129},{129,257},{257,385},{2,130},{1... | collective-permute-start | bytes 884744 | tf_op jit(solution)/shard_map/while/body/eval_jaxpr/ppermute | solution.py:19
  768.7 60.3 %all-reduce.2.cloned.1.call-done = bf16[4,144,144]{2,1,0:T(8,128)(2,1)} async-done(((bf16[4,144,144]{2,1,0:T(8,128)(2,1)}), bf16[4,144,144]{2,1,0:T(8,128)(2,1)}) %all-reduce.2.cloned.1.call-update) | async-done | bytes 165904 | tf_op jit(solution)/shard_map/psum | solution.py:24
  829.9 11.0 %gather_fusion.3 = bf16[3072,144]{1,0:T(8,128)(2,1)S(1)} fusion(bf16[144,144]{1,0:T(8,128)(2,1)S(1)} %fusion.90, s32[3072]{0:T(1024)S(1)} %broadcast_clamp_fusion), kind=kCustom, calls=%fused_computation.3 | custom fusion | bytes 1781760 | tf_op jit(solution)/shard_map/jit(_take)/gather | solution.py:174
  843.4 15.2 %all-to-all-start.1 = ((bf16[1,128,24,144]{3,2,0,1:T(8,128)(2,1)}), bf16[1,128,24,144]{3,2,0,1:T(8,128)(2,1)S(1)}, u32[]{:S(2)}, u32[]{:S(2)}) async-start(bf16[1,128,24,144]{3,2,0,1:T(8,128)(2,1)} %select_multiply_fusion), calls=%async_computation.1 | async-start | bytes 3145728 | tf_op jit(solution)/shard_map/all_to_all | solution.py:178
  862.2 38.7 %all-to-all-done.1 = bf16[1,128,24,144]{3,2,0,1:T(8,128)(2,1)S(1)} async-done(((bf16[1,128,24,144]{3,2,0,1:T(8,128)(2,1)}), bf16[1,128,24,144]{3,2,0,1:T(8,128)(2,1)S(1)}, u32[]{:S(2)}, u32[]{:S(2)}) %all-to-all-start.1) | async-done | bytes 884768 | tf_op jit(solution)/shard_map/all_to_all | solution.py:178
  (148 shorter events, 68.8 us)
Async XLA Ops:
  7.2 611.1 %all-gather.3.cloned.1.call-start = ((), (), s32[]{:S(2)}) async-start(), calls=%async_computation.3 | async-start | bytes 8454144 | tf_op jit(solution)/shard_map/all_gather | solution.py:106
  34.4 18.5 %copy-start.1 = (bf16[2,1024]{1,0:T(2,128)(2,1)S(1)}, bf16[2,1024]{1,0:T(2,128)(2,1)}, u32[]{:S(2)}) copy-start(bf16[2,1024]{1,0:T(2,128)(2,1)} %param.19) | copy-start | bytes 12292
  34.4 20.8 %copy-start = (bf16[1024,144]{0,1:T(8,128)(2,1)S(1)}, bf16[1024,144]{0,1:T(8,128)(2,1)}, u32[]{:S(2)}) copy-start(bf16[1024,144]{0,1:T(8,128)(2,1)} %param.23) | copy-start | bytes 884740
  34.4 66.0 %all-to-all-start = ((bf16[1,128,24,144]{3,2,0,1:T(8,128)(2,1)}), bf16[1,128,24,144]{3,2,0,1:T(8,128)(2,1)S(1)}, u32[]{:S(2)}, u32[]{:S(2)}) async-start(bf16[1,128,24,144]{3,2,0,1:T(8,128)(2,1)} %select_multiply_fusion.1), calls=%async_computation | async-start | bytes 3145728 | tf_op jit(solution)/shard_map/all_to_all | solution.py:89
  52.8 776.2 %all-reduce.2.cloned.1.call-start = ((), (), s32[]{:S(2)}) async-start(), calls=%async_computation.2 | async-start | bytes 589824 | tf_op jit(solution)/shard_map/psum | solution.py:24
  618.2 12.9 %copy-start.3 = (f32[1,1024]{1,0:T(1,128)S(1)}, f32[1,1024]{1,0:T(1,128)}, u32[]{:S(2)}) copy-start(f32[1,1024]{1,0:T(1,128)} %param.22) | copy-start | bytes 12292
  644.8 2.7 collective-permute-start
  661.8 3.4 collective-permute-start
  679.6 5.6 collective-permute-start
  699.5 9.5 %collective-permute-start = (bf16[144,1024]{1,0:T(8,128)(2,1)}, bf16[144,1024]{1,0:T(8,128)(2,1)S(1)}, u32[]{:S(2)}, u32[]{:S(2)}) collective-permute-start(bf16[144,1024]{1,0:T(8,128)(2,1)} %get-tuple-element.624), channel_id=1, source_target_pairs={{0,128},{128,256},{256,384},{1,129},{129,257},{257,385},{2,130},{1... | collective-permute-start | bytes 884744 | tf_op jit(solution)/shard_map/while/body/eval_jaxpr/ppermute | solution.py:19
  709.8 23.0 %collective-permute-start = (bf16[144,1024]{1,0:T(8,128)(2,1)}, bf16[144,1024]{1,0:T(8,128)(2,1)S(1)}, u32[]{:S(2)}, u32[]{:S(2)}) collective-permute-start(bf16[144,1024]{1,0:T(8,128)(2,1)} %get-tuple-element.624), channel_id=1, source_target_pairs={{0,128},{128,256},{256,384},{1,129},{129,257},{257,385},{2,130},{1... | collective-permute-start | bytes 884744 | tf_op jit(solution)/shard_map/while/body/eval_jaxpr/ppermute | solution.py:19
  733.7 9.8 %collective-permute-start = (bf16[144,1024]{1,0:T(8,128)(2,1)}, bf16[144,1024]{1,0:T(8,128)(2,1)S(1)}, u32[]{:S(2)}, u32[]{:S(2)}) collective-permute-start(bf16[144,1024]{1,0:T(8,128)(2,1)} %get-tuple-element.624), channel_id=1, source_target_pairs={{0,128},{128,256},{256,384},{1,129},{129,257},{257,385},{2,130},{1... | collective-permute-start | bytes 884744 | tf_op jit(solution)/shard_map/while/body/eval_jaxpr/ppermute | solution.py:19
  744.2 23.0 %collective-permute-start = (bf16[144,1024]{1,0:T(8,128)(2,1)}, bf16[144,1024]{1,0:T(8,128)(2,1)S(1)}, u32[]{:S(2)}, u32[]{:S(2)}) collective-permute-start(bf16[144,1024]{1,0:T(8,128)(2,1)} %get-tuple-element.624), channel_id=1, source_target_pairs={{0,128},{128,256},{256,384},{1,129},{129,257},{257,385},{2,130},{1... | collective-permute-start | bytes 884744 | tf_op jit(solution)/shard_map/while/body/eval_jaxpr/ppermute | solution.py:19
  843.4 15.8 %copy-start.2 = (s32[128]{0:T(128)S(1)}, s32[128]{0:T(128)}, u32[]{:S(2)}) copy-start(s32[128]{0:T(128)} %param.18) | copy-start | bytes 1540
  843.4 57.5 %all-to-all-start.1 = ((bf16[1,128,24,144]{3,2,0,1:T(8,128)(2,1)}), bf16[1,128,24,144]{3,2,0,1:T(8,128)(2,1)S(1)}, u32[]{:S(2)}, u32[]{:S(2)}) async-start(bf16[1,128,24,144]{3,2,0,1:T(8,128)(2,1)} %select_multiply_fusion), calls=%async_computation.1 | async-start | bytes 3145728 | tf_op jit(solution)/shard_map/all_to_all | solution.py:178
Sparse Core Ops, SparseCore 0:
  10.1 608.1 all-gather.2
  768.8 60.1 all-reduce.1
where the time goes:
time: 911 us; the launch traced here: 910 us
  waiting for transfers between devices  663 us (73%)
  starting transfers between devices  101 us (11%)
  local copies, waits for them, and re-layouts  55.6 us (6%)
  matrix products  50.5 us (6%)
  between operations  16.9 us (2%)
  other arithmetic  14 us (2%)
    all_gather x1, waiting for transfers between devices, per_device(): weight = lax.all_gather(attn_weight[0], 'lat', axis=1, tiled=True)  509 us
    ppermute x7, starting transfers between devices, shifted(): return lax.ppermute(value, axis, pairs)  67.2 us
    psum x1, waiting for transfers between devices, from_root(): return lax.psum(jnp.where(mine, value, jnp.zeros_like(value)), axis)  60.3 us
    all_to_all x1, waiting for transfers between devices, per_device(): lax.all_to_all(outgoing, 'lat', split_axis=1, concat_axis=1, tiled=True)  44.9 us
    all_to_all x1, waiting for transfers between devices, per_device(): lax.all_to_all(returning, 'lat', split_axis=1, concat_axis=1, tiled=True)  38.7 us
    all_to_all x1, starting transfers between devices, per_device(): lax.all_to_all(outgoing, 'lat', split_axis=1, concat_axis=1, tiled=True)  18.4 us
  transfers between devices with their start and end apart: 11, of which 11 were waited for; matrix products, arithmetic and copies ran while one was open for 3% of the time, Pallas kernels for 0%

commit v1 on v0

v1 whole, which is shorter than its diff:
```python
import functools
import math

import jax
import jax.numpy as jnp
from jax import lax
from jax.experimental import pallas as pl
from jax.experimental.pallas import tpu as pltpu
from jax.sharding import Mesh
from jax.sharding import PartitionSpec as P

HEAD_DIM = 64
LEV = 2
WIN_ROWS = 12
WIN_COLS = 6
WTOK = 144
FEAT = 144
LW = 7
PIECE = WIN_COLS * LEV * FEAT
PACK = 16
BF = jnp.bfloat16
F32 = jnp.float32
LAT = ("z", "y", "xl")
DOUBLING = (4, 2, 1)
OFFS = (0, 4, 2, 6, 1, 5, 3, 7)
MIB = 1 << 20

VMEM = pl.BlockSpec(memory_space=pltpu.VMEM)
SMEM = pl.BlockSpec(memory_space=pltpu.SMEM)
ANY = pl.BlockSpec(memory_space=pl.ANY)


def ring(value, axis, by):
    n = lax.axis_size(axis)
    return lax.ppermute(value, axis, [(i, (i + by) % n) for i in range(n)])


def swap(value, axis, bit):
    n = lax.axis_size(axis)
    return lax.ppermute(value, axis, [(i, i ^ bit) for i in range(n)])


def pack_kernel(table, rows_ref, out_ref):
    @pl.loop(0, table.shape[0])
    def _(j):
        column = lax.rem(jnp.maximum(table[j], 0), LW)
        out_ref[2 * j] = rows_ref[column]
        out_ref[2 * j + 1] = rows_ref[LW + column]


def pick_kernel(where, bands, table, came_ref, out_ref):
    window = table[where[0]]
    first = WIN_ROWS * lax.div(jnp.maximum(window, 0), LW) - WIN_ROWS // 2
    out_ref[...] = jnp.zeros_like(out_ref)

    def band(i, start):
        row = start - first
        count = bands[i]

        @pl.when((window >= 0) & (row >= 0) & (row < WIN_ROWS))
        def _():
            out_ref[row] = came_ref[2 * i]

        @pl.when((window >= 0) & (count > 1) & (row >= -1) & (row < WIN_ROWS - 1))
        def _():
            out_ref[row + 1] = came_ref[2 * i + 1]

        return start + count

    lax.fori_loop(0, bands.shape[0], band, jnp.int32(0))


def unpick_kernel(where, bands, table, rows_ref, out_ref):
    window = table[where[0]]
    first = WIN_ROWS * lax.div(jnp.maximum(window, 0), LW) - WIN_ROWS // 2

    def band(i, start):
        row = start - first
        out_ref[2 * i] = rows_ref[jnp.clip(row, 0, WIN_ROWS - 1)]
        out_ref[2 * i + 1] = rows_ref[jnp.clip(row + 1, 0, WIN_ROWS - 1)]
        return start + bands[i]

    lax.fori_loop(0, bands.shape[0], band, jnp.int32(0))


def unpack_kernel(where, bands, table, came_ref, out_ref):
    mine = where[0]
    start = lax.fori_loop(0, mine, lambda i, total: total + bands[i], jnp.int32(0))
    count = bands[mine]
    wide = lax.div(start + WIN_ROWS // 2, WIN_ROWS)
    wide_next = lax.div(start + 1 + WIN_ROWS // 2, WIN_ROWS)
    out_ref[...] = jnp.zeros_like(out_ref)

    @pl.loop(0, table.shape[0])
    def _(j):
        window = table[j]
        across = lax.div(jnp.maximum(window, 0), LW)
        column = lax.rem(jnp.maximum(window, 0), LW)

        @pl.when((window >= 0) & (across == wide))
        def _():
            out_ref[column] = came_ref[2 * j]

        @pl.when((window >= 0) & (count > 1) & (across == wide_next))
        def _():
            out_ref[LW + column] = came_ref[2 * j + 1]


def to_rows(tokens):
    rows = tokens.reshape(-1, PIECE)
    return jnp.pad(rows, ((0, 0), (0, PACK * 128 - PIECE))).reshape(-1, PACK, 128)


def from_rows(rows):
    return rows.reshape(-1, PACK * 128)[:, :PIECE].reshape(-1, FEAT)


def join_kernel(pos, *refs):
    out, sem = refs[-2], refs[-1]
    pieces = refs[:-2]
    half = len(pieces) // 2
    z, y = pos[1], pos[2]

    def copies(side, index):
        ref = pieces[side * half + index]
        step = (0, -1, -2, -3, 1, 2, 3, 4, 4)[index]
        subs = range(8) if index < 7 else (range(4) if index == 7 else range(4, 8))
        for slot, sub in enumerate(subs):
            if side == 0:
                plane, line = lax.rem(z + step + 8, 8), y ^ OFFS[sub]
            else:
                plane, line = z ^ OFFS[sub], lax.rem(y + step + 8, 8)
            row = pl.multiple_of((plane * 8 + line) * 64, 64)
            yield pltpu.make_async_copy(
                ref.at[pl.ds(slot * 64, 64)], out.at[side, pl.ds(row, 64)], sem
            )

    every = [c for side in range(2) for i in range(half) for c in copies(side, i)]
    for c in every:
        c.start()
    for c in every:
        c.wait()


def gather_section(weight, pos):
    mine = weight[0].T
    pair = lax.all_gather(mine, "xl", axis=0, tiled=True)
    a, b = pair[:, :512], pair[:, 512:]
    for bit in DOUBLING:
        a_far, b_far = swap(a, "y", bit), swap(b, "z", bit)
        a, b = jnp.concatenate([a, a_far]), jnp.concatenate([b, b_far])
    pieces = []
    chains = [(a, "z", 1), (a, "z", -1), (b, "y", 1), (b, "y", -1)]
    got = [[] for _ in chains]
    held = [c[0] for c in chains]
    for step in range(4):
        for n, (_, axis, by) in enumerate(chains):
            value = held[n]
            if step == 3:
                value = value[:256] if by > 0 else value[256:]
            held[n] = ring(value, axis, by)
            got[n].append(held[n])
    for own, ahead, behind in ((a, got[0], got[1]), (b, got[2], got[3])):
        pieces += [own, *ahead[:3], *behind[:3], ahead[3], behind[3]]
    return pl.pallas_call(
        join_kernel,
        out_shape=jax.ShapeDtypeStruct((2, 4096, 512), BF),
        in_specs=[SMEM] + [ANY] * len(pieces),
        out_specs=ANY,
        scratch_shapes=[pltpu.SemaphoreType.DMA(())],
        name="join",
    )(pos, *pieces)


def matmul_t(left, right):
    return lax.dot_general(left, right, (((1,), (1,)), ((), ())), preferred_element_type=F32)


def block(hidden, gain, weights, wait, allowed):
    wide = hidden.astype(F32)
    scale = lax.rsqrt(jnp.mean(wide * wide, axis=-1, keepdims=True) + 1e-06)
    normed = (wide * scale * gain).astype(BF)

    def project(left, part):
        wait(part)
        rows = slice(1024 * part, 1024 * (part + 1))
        return matmul_t(left[:, :512], weights[0, rows]) + matmul_t(left[:, 512:], weights[1, rows])

    query = (project(normed, 0).astype(BF).astype(F32) * (1 / math.sqrt(HEAD_DIM))).astype(BF)
    keyed = project(normed, 1).astype(BF)
    valued = project(normed, 2).astype(BF)
    low = lax.broadcasted_iota(jnp.int32, (WTOK, 128), 1) < HEAD_DIM
    slabs = hidden.shape[0] // WTOK
    all_mixed = []
    for slab in range(slabs):
        here = slice(WTOK * slab, WTOK * (slab + 1))
        mixed = []
        for two in range(8):
            lanes = slice(128 * two, 128 * (two + 1))
            q2, k2, v2 = query[here, lanes], keyed[here, lanes], valued[here, lanes]
            outs = []
            for part in range(2):
                q1 = jnp.where(low if part == 0 else ~low, q2, jnp.zeros_like(q2))
                scores = jnp.where(allowed, matmul_t(q1, k2), -1e30)
                top = jnp.max(scores, axis=-1, keepdims=True)
                grown = jnp.exp(scores - top)
                probs = (grown / jnp.sum(grown, axis=-1, keepdims=True)).astype(BF)
                outs.append(jnp.dot(probs, v2, preferred_element_type=F32))
            mixed.append(jnp.where(low, outs[0], outs[1]).astype(BF))
        all_mixed.append(jnp.concatenate(mixed, axis=1))
    mixed = jnp.concatenate(all_mixed, axis=0) if slabs > 1 else all_mixed[0]
    return (wide + project(mixed, 3)).astype(BF)


def sections_kernel(
    pos, bands, table, raw_ref, came_ref, embed_ref, level_ref, gain_ref, head_ref, own_ref, other_ref,
    hidden_ref, out_ref, rows_ref, weights, sems,
):
    core, late = pos[3], pos[4]

    def load(source, section):
        for part in range(4):
            rows = pl.ds(1024 * part, 1024)
            pltpu.make_async_copy(
                source.at[:, rows], weights.at[section, :, rows], sems.at[section, part]
            ).start()

    @pl.when(core == 0)
    def _():
        load(own_ref, 0)
        load(other_ref, 1)

    @pl.when(core == 1)
    def _():
        load(other_ref, 0)
        load(own_ref, 1)

    def waiter(section):
        def wait(part):
            rows = pl.ds(1024 * part, 1024)
            pltpu.make_async_copy(
                own_ref.at[:, rows], weights.at[section, :, rows], sems.at[section, part]
            ).wait()

        return wait

    slabs = raw_ref.shape[0]
    query_token = lax.broadcasted_iota(jnp.int32, (WTOK, WTOK), 0)
    key_token = lax.broadcasted_iota(jnp.int32, (WTOK, WTOK), 1)
    half = WIN_ROWS * WIN_COLS
    same = lax.rem(query_token, half) == lax.rem(key_token, half)
    window = table[pos[0]]
    first = WIN_ROWS * lax.div(jnp.maximum(window, 0), LW) - WIN_ROWS // 2
    total_rows = 3 * bands.shape[0] // 2

    def inside(token):
        row = first + lax.rem(lax.div(token, WIN_COLS), WIN_ROWS)
        return (window >= 0) & (row >= 0) & (row < total_rows)

    keep = inside(key_token)
    is_late = late == 1
    first_mask = (same & (late == 0)) | (keep & (late == 1))
    second_mask = (keep & (late == 0)) | (same & (late == 1))
    to_window = (lax.div(query_token, half) == lax.rem(key_token, LEV)) & (
        lax.rem(query_token, half) == lax.div(key_token, LEV)
    )
    from_window = (lax.rem(query_token, LEV) == lax.div(key_token, half)) & (
        lax.div(query_token, LEV) == lax.rem(key_token, half)
    )
    to_window = to_window.astype(BF)
    from_window = from_window.astype(BF)
    upper = lax.broadcasted_iota(jnp.int32, (WTOK, 1), 0) < half
    level_rows = jnp.where(upper, level_ref[0:1].astype(F32), level_ref[1:2].astype(F32))
    starts = []
    for slab in range(slabs):
        raw = jnp.dot(to_window, raw_ref[slab], preferred_element_type=F32).astype(BF)
        embedded = (jnp.dot(raw, embed_ref[...], preferred_element_type=F32) + level_rows).astype(BF)
        starts.append(jnp.where(is_late, came_ref[slab], embedded))
    hidden = jnp.concatenate(starts, axis=0) if slabs > 1 else starts[0]
    hidden = block(hidden, gain_ref[0:1], weights.at[0], waiter(0), first_mask)
    hidden = block(hidden, gain_ref[1:2], weights.at[1], waiter(1), second_mask)
    result = jnp.dot(hidden, head_ref[...], preferred_element_type=F32)
    keep_row = inside(lax.broadcasted_iota(jnp.int32, (WTOK, 1), 0))
    for slab in range(slabs):
        here = slice(WTOK * slab, WTOK * (slab + 1))
        hidden_ref[slab] = hidden[here]
        out = jnp.where(keep_row, result[here], 0.0).astype(BF)
        out_ref[slab] = out
        rows_ref[slab] = jnp.dot(from_window, out, preferred_element_type=F32).astype(BF)


def two_sections(pos, bands, table, raw, came, embed, level, gains, head, own, other):
    slabs = raw.shape[0]
    width = embed.shape[1]
    return pl.pallas_call(
        sections_kernel,
        out_shape=(
            jax.ShapeDtypeStruct((slabs, WTOK, width), BF),
            jax.ShapeDtypeStruct((slabs, WTOK, FEAT), BF),
            jax.ShapeDtypeStruct((slabs, WTOK, FEAT), BF),
        ),
        in_specs=[SMEM] * 3 + [VMEM] * 6 + [ANY] * 2,
        out_specs=(VMEM,) * 3,
        scratch_shapes=[
            pltpu.VMEM((2, 2, 4096, 512), BF),
            pltpu.SemaphoreType.DMA((2, 4)),
        ],
        compiler_params=pltpu.CompilerParams(vmem_limit_bytes=48 * MIB),
        name="sections",
    )(pos, bands, table, raw, came, embed, level, gains, head, own, other)


def small_call(body, out_rows, scalars, value, name):
    return pl.pallas_call(
        body,
        out_shape=jax.ShapeDtypeStruct((out_rows, PACK, 128), BF),
        in_specs=[SMEM] * len(scalars) + [VMEM],
        out_specs=VMEM,
        name=name,
    )(*scalars, value)


def per_device(
    fields, band_rows, window_table, level_embed, embed_weight, attn_weight, norm_gain, head_weight
):
    late, core = lax.axis_index("xh"), lax.axis_index("c")
    pos = jnp.stack([lax.axis_index(LAT), lax.axis_index("z"), lax.axis_index("y"), core, late])
    scalars = (pos, band_rows, window_table)
    lat_count = band_rows.shape[0]
    is_late = late == 1

    message = small_call(pack_kernel, 2 * lat_count, (window_table,), to_rows(fields[0]), "pack")
    arrived = lax.all_to_all(message, LAT, 0, 0, tiled=True)
    raw_rows = small_call(pick_kernel, WIN_ROWS, scalars, arrived, "pick")
    own_raw = from_rows(raw_rows)
    far_raw = swap(own_raw, "xh", 1)

    own = gather_section(attn_weight, pos)
    other = swap(own, "c", 1)
    gains = lax.all_gather(norm_gain, "c", axis=0, tiled=True)

    run = functools.partial(
        two_sections,
        pos,
        band_rows,
        window_table,
        embed=embed_weight,
        level=level_embed,
        gains=gains,
        head=head_weight,
        own=own,
        other=other,
    )
    idle = jnp.zeros((1, WTOK, embed_weight.shape[1]), BF)
    h1, _, _ = run(own_raw[None], idle)
    c1 = swap(h1, "xh", 1)
    h2, _, _ = run(far_raw[None], h1)
    c2 = swap(h2, "xh", 1)
    _, out1, rows1 = run(far_raw[None], c1)
    back1, back_rows1 = swap(out1, "xh", 1), swap(rows1, "xh", 1)
    _, out2, rows2 = run(far_raw[None], c2)
    window_decoded = jnp.where(is_late, out2, back1)
    own_rows = jnp.where(is_late, rows2, back_rows1)

    reply = small_call(unpick_kernel, 2 * lat_count, scalars, to_rows(own_rows[0]), "unpick")
    came_back = lax.all_to_all(reply, LAT, 0, 0, tiled=True)
    decoded_rows = small_call(unpack_kernel, 2 * LW, scalars, came_back, "unpack")
    decoded = from_rows(decoded_rows)[None]
    return (decoded, window_decoded)


def solution(mesh):
    fine = Mesh(mesh.devices.reshape(2, 2, 8, 8, 2), ("xh", "c", "z", "y", "xl"))
    segment = ("xh", "c")
    placed = (
        P(segment, LAT, None),
        P(),
        P(),
        P(),
        P(),
        P(segment, None, LAT),
        P(segment, None),
        P(),
    )
    return jax.shard_map(
        per_device,
        mesh=fine,
        in_specs=placed,
        out_specs=(P(segment, LAT, None), P(segment, LAT, None)),
        check_vma=False,
    )
```

time: 911 us -> 536 us (0.59)
  the two profiles are of different devices: /device:TPU:10 before, /device:TPU:8 now
where the time goes in v1:
time: 536 us; the launch traced here: 534 us
  Pallas kernels  325 us (61%)
  starting transfers between devices  125 us (23%)
  waiting for transfers between devices  64.1 us (12%)
  local copies, waits for them, and re-layouts  11.5 us (2%)
  blocking collectives  6.95 us (1%)
    pallas_call x1, Pallas kernels, gather_section(): pl.pallas_call(join_kernel, out_shape=jax.ShapeDtypeStruct((2, 4096, 512)...  256 us
    ppermute x12, starting transfers between devices, swap(): return lax.ppermute(value, axis, [(i, i ^ bit) for i in range(n)])  55.2 us
    pallas_call x4, Pallas kernels, two_sections(): pl.pallas_call(sections_kernel, out_shape=(jax.ShapeDtypeStruct((slabs, W...  52 us
    ppermute x16, starting transfers between devices, ring(): return lax.ppermute(value, axis, [(i, (i + by) % n) for i in range(n)])  50 us
    all_to_all x1, waiting for transfers between devices, per_device(): arrived = lax.all_to_all(message, LAT, 0, 0, tiled=True)  28.7 us
    all_to_all x1, waiting for transfers between devices, per_device(): came_back = lax.all_to_all(reply, LAT, 0, 0, tiled=True)  20.2 us
    pallas_call x4, Pallas kernels, small_call(): pl.pallas_call(body, out_shape=jax.ShapeDtypeStruct((out_rows, PACK, 128)...  16.8 us
    all_to_all x1, starting transfers between devices, per_device(): arrived = lax.all_to_all(message, LAT, 0, 0, tiled=True)  12.6 us
  transfers between devices with their start and end apart: 30, of which 10 were waited for; matrix products, arithmetic and copies ran while one was open for 1% of the time, Pallas kernels for 11%

profile of v1, /device:TPU:8, one launch (start us, length us, event | category | flops | bytes accessed | tf_op | source)
XLA Modules:
  0.0 534.1 jit_solution(1544855552357815277)
XLA Ops:
  0.6 5.2 all_gather.7
  5.8 6.8 %collective-permute-start.1 = (bf16[64,512]{1,0:T(8,128)(2,1)S(1)}, bf16[64,512]{1,0:T(8,128)(2,1)S(1)}, u32[]{:S(2)}, u32[]{:S(2)}) collective-permute-start(bf16[64,512]{1,0:T(8,128)(2,1)S(1)} %get-tuple-element.19), channel_id=1, source_target_pairs={{0,8},{2,10},{4,12},{6,14},{8,0},{10,2},{12,4},{14,6},{1,9},{3,11}... | collective-permute-start | bytes 196616 | tf_op jit(solution)/shard_map/ppermute | solution.py:40
  12.6 10.9 %collective-permute-start.12 = (bf16[64,512]{1,0:T(8,128)(2,1)S(1)}, bf16[64,512]{1,0:T(8,128)(2,1)S(1)}, u32[]{:S(2)}, u32[]{:S(2)}) collective-permute-start(bf16[64,512]{1,0:T(8,128)(2,1)S(1)} %get-tuple-element.18), channel_id=1, source_target_pairs={{0,64},{16,80},{32,96},{48,112},{64,0},{80,16},{96,32},{112,48},{1... | collective-permute-start | bytes 196616 | tf_op jit(solution)/shard_map/ppermute | solution.py:40
  26.3 4.6 collective-permute-start.13
  31.5 4.6 collective-permute-start.3
  36.1 3.4 collective-permute-start.14
  40.4 4.4 collective-permute-start.7
  47.1 3.1 collective-permute-start.18
  55.1 4.2 collective-permute-start.8
  61.2 3.3 collective-permute-start.19
  67.6 5.3 collective-permute-start.9
  74.9 3.3 collective-permute-start.20
  81.6 5.1 collective-permute-start.11
  90.2 3.7 collective-permute-start.22
  98.8 5.7 %collective-permute-done.21.refs_16_ = bf16[256,512]{1,0:T(8,128)(2,1)} collective-permute-done((bf16[256,512]{1,0:T(8,128)(2,1)}, bf16[256,512]{1,0:T(8,128)(2,1)}, u32[]{:S(2)}, u32[]{:S(2)}) %collective-permute-start.21) | collective-permute-done | bytes 262176 | tf_op jit(solution)/shard_map/ppermute | solution.py:35
  104.6 255.9 %join.1.own_ref = bf16[2,4096,512]{2,1,0:T(8,128)(2,1)} custom-call(s32[5]{0:T(128)} %stack.23.where.pos, bf16[512,512]{1,0:T(8,128)(2,1)} %copy-done.7, bf16[512,512]{1,0:T(8,128)(2,1)} %copy-done.14, bf16[512,512]{1,0:T(8,128)(2,1)} %copy-done.18, bf16[512,512]{1,0:T(8,128)(2,1)} %copy-done.10, bf16[512,512]{1,0:T(8,128)(2,1)} %copy-done.13, ...), custom_call_target="tpu_custom_call" | custom-call | tf_op jit(solution)/shard_map/join/pallas_call | solution.py:165
  363.4 3.4 pack.1
  366.8 12.6 %all-to-all-start = ((bf16[256,16,128]{2,1,0:T(8,128)(2,1)}), bf16[256,16,128]{2,1,0:T(8,128)(2,1)S(1)}, u32[]{:S(2)}, u32[]{:S(2)}) async-start(bf16[256,16,128]{2,1,0:T(8,128)(2,1)} %pack.1), calls=%async_computation | async-start | bytes 2097152 | tf_op jit(solution)/shard_map/all_to_all | solution.py:333
  382.4 28.7 %all-to-all-done.came_ref = bf16[256,16,128]{2,1,0:T(8,128)(2,1)S(1)} async-done(((bf16[256,16,128]{2,1,0:T(8,128)(2,1)}), bf16[256,16,128]{2,1,0:T(8,128)(2,1)S(1)}, u32[]{:S(2)}, u32[]{:S(2)}) %all-to-all-start) | async-done | bytes 1048608 | tf_op jit(solution)/shard_map/all_to_all | solution.py:333
  412.1 4.7 pick.1
  417.9 4.8 collective-permute-start
  422.8 13.0 %sections.4 = (bf16[1,144,1024]{2,1,0:T(8,128)(2,1)S(1)}, bf16[1,144,144]{2,1,0:T(8,128)(2,1)}, bf16[1,144,144]{2,1,0:T(8,128)(2,1)}) custom-call(s32[5]{0:T(128)S(1)} %copy-done.2, s32[128]{0:T(128)S(1)} %copy-done.4, s32[128]{0:T(128)S(1)} %copy-done.3, bf16[1,144,144]{2,1,0:T(8,128)(2,1)S(1)} %broadcast_in_dim_reshape.6.raw_ref, ...), custom_call_target="tpu_custom_call" | custom-call | tf_op jit(solution)/shard_map/sections/pallas_call | solution.py:295
  438.8 13.0 %sections.5 = (bf16[1,144,1024]{2,1,0:T(8,128)(2,1)S(1)}, bf16[1,144,144]{2,1,0:T(8,128)(2,1)}, bf16[1,144,144]{2,1,0:T(8,128)(2,1)}) custom-call(s32[5]{0:T(128)S(1)} %copy-done.2, s32[128]{0:T(128)S(1)} %copy-done.4, s32[128]{0:T(128)S(1)} %copy-done.3, bf16[1,144,144]{2,1,0:T(8,128)(2,1)S(1)} %bitcast.25, ...), custom_call_target="tpu_custom_call" | custom-call | tf_op jit(solution)/shard_map/sections/pallas_call | solution.py:295
  451.9 4.9 collective-permute-start.24
  456.8 13.0 %sections.7 = (bf16[1,144,1024]{2,1,0:T(8,128)(2,1)}, bf16[1,144,144]{2,1,0:T(8,128)(2,1)S(1)}, bf16[1,144,144]{2,1,0:T(8,128)(2,1)S(1)}) custom-call(s32[5]{0:T(128)S(1)} %copy-done.2, s32[128]{0:T(128)S(1)} %copy-done.4, s32[128]{0:T(128)S(1)} %copy-done.3, bf16[1,144,144]{2,1,0:T(8,128)(2,1)S(1)} %bitcast.26, ...), custom_call_target="tpu_custom_call" | custom-call | tf_op jit(solution)/shard_map/sections/pallas_call | solution.py:295
  472.8 13.0 %sections.6 = (bf16[1,144,1024]{2,1,0:T(8,128)(2,1)}, bf16[1,144,144]{2,1,0:T(8,128)(2,1)S(1)}, bf16[1,144,144]{2,1,0:T(8,128)(2,1)S(1)}) custom-call(s32[5]{0:T(128)S(1)} %copy-done.2, s32[128]{0:T(128)S(1)} %copy-done.4, s32[128]{0:T(128)S(1)} %copy-done.3, bf16[1,144,144]{2,1,0:T(8,128)(2,1)S(1)} %bitcast.27, ...), custom_call_target="tpu_custom_call" | custom-call | tf_op jit(solution)/shard_map/sections/pallas_call | solution.py:295
  486.6 3.2 unpick.1
  489.8 6.7 %all-to-all-start.1 = ((bf16[256,16,128]{2,1,0:T(8,128)(2,1)}), bf16[256,16,128]{2,1,0:T(8,128)(2,1)S(1)}, u32[]{:S(2)}, u32[]{:S(2)}) async-start(bf16[256,16,128]{2,1,0:T(8,128)(2,1)} %unpick.1), calls=%async_computation.1 | async-start | bytes 2097152 | tf_op jit(solution)/shard_map/all_to_all | solution.py:366
  496.5 4.6 collective-permute-start.27
  501.2 3.8 collective-permute-done.27
  505.6 20.2 %all-to-all-done.1.came_ref = bf16[256,16,128]{2,1,0:T(8,128)(2,1)S(1)} async-done(((bf16[256,16,128]{2,1,0:T(8,128)(2,1)}), bf16[256,16,128]{2,1,0:T(8,128)(2,1)S(1)}, u32[]{:S(2)}, u32[]{:S(2)}) %all-to-all-start.1) | async-done | bytes 1048608 | tf_op jit(solution)/shard_map/all_to_all | solution.py:366
  526.9 5.5 %unpack.1 = bf16[14,16,128]{2,1,0:T(8,128)(2,1)} custom-call(s32[5]{0:T(128)} %stack.23.where.pos, s32[128]{0:T(128)} %bands.13, s32[128]{0:T(128)} %table.15, bf16[256,16,128]{2,1,0:T(8,128)(2,1)} %copy-done.5), custom_call_target="tpu_custom_call" | custom-call | tf_op jit(solution)/shard_map/unpack/pallas_call | solution.py:314
  (121 shorter events, 48.0 us)
Async XLA Ops:
  5.8 17.8 %collective-permute-start.1 = (bf16[64,512]{1,0:T(8,128)(2,1)S(1)}, bf16[64,512]{1,0:T(8,128)(2,1)S(1)}, u32[]{:S(2)}, u32[]{:S(2)}) collective-permute-start(bf16[64,512]{1,0:T(8,128)(2,1)S(1)} %get-tuple-element.19), channel_id=1, source_target_pairs={{0,8},{2,10},{4,12},{6,14},{8,0},{10,2},{12,4},{14,6},{1,9},{3,11}... | collective-permute-start | bytes 196616 | tf_op jit(solution)/shard_map/ppermute | solution.py:40
  12.6 13.7 %collective-permute-start.12 = (bf16[64,512]{1,0:T(8,128)(2,1)S(1)}, bf16[64,512]{1,0:T(8,128)(2,1)S(1)}, u32[]{:S(2)}, u32[]{:S(2)}) collective-permute-start(bf16[64,512]{1,0:T(8,128)(2,1)S(1)} %get-tuple-element.18), channel_id=1, source_target_pairs={{0,64},{16,80},{32,96},{48,112},{64,0},{80,16},{96,32},{112,48},{1... | collective-permute-start | bytes 196616 | tf_op jit(solution)/shard_map/ppermute | solution.py:40
  23.6 7.9 %collective-permute-start.2 = (bf16[128,512]{1,0:T(8,128)(2,1)S(1)}, bf16[128,512]{1,0:T(8,128)(2,1)S(1)}, u32[]{:S(2)}, u32[]{:S(2)}) collective-permute-start(bf16[128,512]{1,0:T(8,128)(2,1)S(1)} %pad_maximum_fusion.4), channel_id=1, source_target_pairs={{0,4},{2,6},{4,0},{6,2},{8,12},{10,14},{12,8},{14,10},{1,5},{3,7},... | collective-permute-start | bytes 393224 | tf_op jit(solution)/shard_map/ppermute | solution.py:40
  26.3 9.7 %collective-permute-start.13 = (bf16[128,512]{1,0:T(8,128)(2,1)S(1)}, bf16[128,512]{1,0:T(8,128)(2,1)S(1)}, u32[]{:S(2)}, u32[]{:S(2)}) collective-permute-start(bf16[128,512]{1,0:T(8,128)(2,1)S(1)} %pad_maximum_fusion.5), channel_id=1, source_target_pairs={{0,32},{16,48},{32,0},{48,16},{64,96},{80,112},{96,64},{112,80},{1... | collective-permute-start | bytes 393224 | tf_op jit(solution)/shard_map/ppermute | solution.py:40
  31.5 8.9 %collective-permute-start.3 = (bf16[256,512]{1,0:T(8,128)(2,1)S(1)}, bf16[256,512]{1,0:T(8,128)(2,1)S(1)}, u32[]{:S(2)}, u32[]{:S(2)}) collective-permute-start(bf16[256,512]{1,0:T(8,128)(2,1)S(1)} %pad_maximum_fusion.2), channel_id=1, source_target_pairs={{0,2},{2,0},{4,6},{6,4},{8,10},{10,8},{12,14},{14,12},{1,3},{3,1},... | collective-permute-start | bytes 786440 | tf_op jit(solution)/shard_map/ppermute | solution.py:40
  36.1 11.0 %collective-permute-start.14 = (bf16[256,512]{1,0:T(8,128)(2,1)S(1)}, bf16[256,512]{1,0:T(8,128)(2,1)S(1)}, u32[]{:S(2)}, u32[]{:S(2)}) collective-permute-start(bf16[256,512]{1,0:T(8,128)(2,1)S(1)} %pad_maximum_fusion.3), channel_id=1, source_target_pairs={{0,16},{16,0},{32,48},{48,32},{64,80},{80,64},{96,112},{112,96},{1... | collective-permute-start | bytes 786440 | tf_op jit(solution)/shard_map/ppermute | solution.py:40
  40.4 14.6 %collective-permute-start.7 = (bf16[512,512]{1,0:T(8,128)(2,1)S(1)}, bf16[512,512]{1,0:T(8,128)(2,1)S(1)}, u32[]{:S(2)}, u32[]{:S(2)}) collective-permute-start(bf16[512,512]{1,0:T(8,128)(2,1)S(1)} %pad_maximum_fusion.refs_0_), channel_id=1, source_target_pairs={{0,112},{16,0},{32,16},{48,32},{64,48},{80,64},{96,80},{112,96},{1... | collective-permute-start | bytes 1572872 | tf_op jit(solution)/shard_map/ppermute | solution.py:35
  44.9 14.4 %collective-permute-start.4 = (bf16[512,512]{1,0:T(8,128)(2,1)S(1)}, bf16[512,512]{1,0:T(8,128)(2,1)S(1)}, u32[]{:S(2)}, u32[]{:S(2)}) collective-permute-start(bf16[512,512]{1,0:T(8,128)(2,1)S(1)} %pad_maximum_fusion.refs_0_), channel_id=1, source_target_pairs={{0,16},{16,32},{32,48},{48,64},{64,80},{80,96},{96,112},{112,0},{1... | collective-permute-start | bytes 1572872 | tf_op jit(solution)/shard_map/ppermute | solution.py:35
  47.1 14.1 %collective-permute-start.18 = (bf16[512,512]{1,0:T(8,128)(2,1)S(1)}, bf16[512,512]{1,0:T(8,128)(2,1)S(1)}, u32[]{:S(2)}, u32[]{:S(2)}) collective-permute-start(bf16[512,512]{1,0:T(8,128)(2,1)S(1)} %pad_maximum_fusion.1.refs_9_), channel_id=1, source_target_pairs={{0,14},{2,0},{4,2},{6,4},{8,6},{10,8},{12,10},{14,12},{1,15},{3,1}... | collective-permute-start | bytes 1572872 | tf_op jit(solution)/shard_map/ppermute | solution.py:35
  50.3 14.2 %collective-permute-start.15 = (bf16[512,512]{1,0:T(8,128)(2,1)S(1)}, bf16[512,512]{1,0:T(8,128)(2,1)S(1)}, u32[]{:S(2)}, u32[]{:S(2)}) collective-permute-start(bf16[512,512]{1,0:T(8,128)(2,1)S(1)} %pad_maximum_fusion.1.refs_9_), channel_id=1, source_target_pairs={{0,2},{2,4},{4,6},{6,8},{8,10},{10,12},{12,14},{14,0},{1,3},{3,5},... | collective-permute-start | bytes 1572872 | tf_op jit(solution)/shard_map/ppermute | solution.py:35
  55.1 12.6 %collective-permute-start.8 = (bf16[512,512]{1,0:T(8,128)(2,1)S(1)}, bf16[512,512]{1,0:T(8,128)(2,1)S(1)}, u32[]{:S(2)}, u32[]{:S(2)}) collective-permute-start(bf16[512,512]{1,0:T(8,128)(2,1)S(1)} %collective-permute-done.7.refs_4_), channel_id=1, source_target_pairs={{0,112},{16,0},{32,16},{48,32},{64,48},{80,64},{96,80},{112,96},{1... | collective-permute-start | bytes 1572872 | tf_op jit(solution)/shard_map/ppermute | solution.py:35
  59.3 13.6 %collective-permute-start.5 = (bf16[512,512]{1,0:T(8,128)(2,1)S(1)}, bf16[512,512]{1,0:T(8,128)(2,1)S(1)}, u32[]{:S(2)}, u32[]{:S(2)}) collective-permute-start(bf16[512,512]{1,0:T(8,128)(2,1)S(1)} %collective-permute-done.4.refs_1_), channel_id=1, source_target_pairs={{0,16},{16,32},{32,48},{48,64},{64,80},{80,96},{96,112},{112,0},{1... | collective-permute-start | bytes 1572872 | tf_op jit(solution)/shard_map/ppermute | solution.py:35
  61.2 13.6 %collective-permute-start.19 = (bf16[512,512]{1,0:T(8,128)(2,1)S(1)}, bf16[512,512]{1,0:T(8,128)(2,1)S(1)}, u32[]{:S(2)}, u32[]{:S(2)}) collective-permute-start(bf16[512,512]{1,0:T(8,128)(2,1)S(1)} %collective-permute-done.18.refs_13_), channel_id=1, source_target_pairs={{0,14},{2,0},{4,2},{6,4},{8,6},{10,8},{12,10},{14,12},{1,15},{3,1}... | collective-permute-start | bytes 1572872 | tf_op jit(solution)/shard_map/ppermute | solution.py:35
  64.5 13.6 %collective-permute-start.16 = (bf16[512,512]{1,0:T(8,128)(2,1)S(1)}, bf16[512,512]{1,0:T(8,128)(2,1)S(1)}, u32[]{:S(2)}, u32[]{:S(2)}) collective-permute-start(bf16[512,512]{1,0:T(8,128)(2,1)S(1)} %collective-permute-done.15.refs_10_), channel_id=1, source_target_pairs={{0,2},{2,4},{4,6},{6,8},{8,10},{10,12},{12,14},{14,0},{1,3},{3,5},... | collective-permute-start | bytes 1572872 | tf_op jit(solution)/shard_map/ppermute | solution.py:35
  67.6 13.2 %collective-permute-start.9 = (bf16[512,512]{1,0:T(8,128)(2,1)S(1)}, bf16[512,512]{1,0:T(8,128)(2,1)S(1)}, u32[]{:S(2)}, u32[]{:S(2)}) collective-permute-start(bf16[512,512]{1,0:T(8,128)(2,1)S(1)} %collective-permute-done.8.refs_5_), channel_id=1, source_target_pairs={{0,112},{16,0},{32,16},{48,32},{64,48},{80,64},{96,80},{112,96},{1... | collective-permute-start | bytes 1572872 | tf_op jit(solution)/shard_map/ppermute | solution.py:35
  73.0 13.8 %collective-permute-start.6 = (bf16[512,512]{1,0:T(8,128)(2,1)S(1)}, bf16[512,512]{1,0:T(8,128)(2,1)S(1)}, u32[]{:S(2)}, u32[]{:S(2)}) collective-permute-start(bf16[512,512]{1,0:T(8,128)(2,1)S(1)} %collective-permute-done.5.refs_2_), channel_id=1, source_target_pairs={{0,16},{16,32},{32,48},{48,64},{64,80},{80,96},{96,112},{112,0},{1... | collective-permute-start | bytes 1572872 | tf_op jit(solution)/shard_map/ppermute | solution.py:35
  74.9 14.5 %collective-permute-start.20 = (bf16[512,512]{1,0:T(8,128)(2,1)S(1)}, bf16[512,512]{1,0:T(8,128)(2,1)S(1)}, u32[]{:S(2)}, u32[]{:S(2)}) collective-permute-start(bf16[512,512]{1,0:T(8,128)(2,1)S(1)} %collective-permute-done.19.refs_14_), channel_id=1, source_target_pairs={{0,14},{2,0},{4,2},{6,4},{8,6},{10,8},{12,10},{14,12},{1,15},{3,1}... | collective-permute-start | bytes 1572872 | tf_op jit(solution)/shard_map/ppermute | solution.py:35
  78.2 15.8 %collective-permute-start.17 = (bf16[512,512]{1,0:T(8,128)(2,1)S(1)}, bf16[512,512]{1,0:T(8,128)(2,1)S(1)}, u32[]{:S(2)}, u32[]{:S(2)}) collective-permute-start(bf16[512,512]{1,0:T(8,128)(2,1)S(1)} %collective-permute-done.16.refs_11_), channel_id=1, source_target_pairs={{0,2},{2,4},{4,6},{6,8},{8,10},{10,12},{12,14},{14,0},{1,3},{3,5},... | collective-permute-start | bytes 1572872 | tf_op jit(solution)/shard_map/ppermute | solution.py:35
  81.6 15.9 %collective-permute-start.11 = (bf16[256,512]{1,0:T(8,128)(2,1)}, bf16[256,512]{1,0:T(8,128)(2,1)}, u32[]{:S(2)}, u32[]{:S(2)}) collective-permute-start(bf16[256,512]{1,0:T(8,128)(2,1)} %slice.35), channel_id=1, source_target_pairs={{0,112},{16,0},{32,16},{48,32},{64,48},{80,64},{96,80},{112,96},{1... | collective-permute-start | bytes 786440 | tf_op jit(solution)/shard_map/ppermute | solution.py:35
  87.5 10.0 %collective-permute-start.10 = (bf16[256,512]{1,0:T(8,128)(2,1)}, bf16[256,512]{1,0:T(8,128)(2,1)}, u32[]{:S(2)}, u32[]{:S(2)}) collective-permute-start(bf16[256,512]{1,0:T(8,128)(2,1)} %slice.34), channel_id=1, source_target_pairs={{0,16},{16,32},{32,48},{48,64},{64,80},{80,96},{96,112},{112,0},{1... | collective-permute-start | bytes 786440 | tf_op jit(solution)/shard_map/ppermute | solution.py:35
  90.2 8.6 %collective-permute-start.22 = (bf16[256,512]{1,0:T(8,128)(2,1)}, bf16[256,512]{1,0:T(8,128)(2,1)}, u32[]{:S(2)}, u32[]{:S(2)}) collective-permute-start(bf16[256,512]{1,0:T(8,128)(2,1)} %slice.38), channel_id=1, source_target_pairs={{0,14},{2,0},{4,2},{6,4},{8,6},{10,8},{12,10},{14,12},{1,15},{3,1}... | collective-permute-start | bytes 786440 | tf_op jit(solution)/shard_map/ppermute | solution.py:35
  94.8 9.8 %collective-permute-start.21 = (bf16[256,512]{1,0:T(8,128)(2,1)}, bf16[256,512]{1,0:T(8,128)(2,1)}, u32[]{:S(2)}, u32[]{:S(2)}) collective-permute-start(bf16[256,512]{1,0:T(8,128)(2,1)} %slice.37), channel_id=1, source_target_pairs={{0,2},{2,4},{4,6},{6,8},{8,10},{10,12},{12,14},{14,0},{1,3},{3,5},... | collective-permute-start | bytes 786440 | tf_op jit(solution)/shard_map/ppermute | solution.py:35
  97.5 325.3 %copy-start.2 = (s32[5]{0:T(128)S(1)}, s32[5]{0:T(128)}, u32[]{:S(2)}) copy-start(s32[5]{0:T(128)} %stack.23.where.pos) | copy-start | bytes 64
  97.5 325.3 %copy-start.3 = (s32[128]{0:T(128)S(1)}, s32[128]{0:T(128)}, u32[]{:S(2)}) copy-start(s32[128]{0:T(128)} %table.15) | copy-start | bytes 1540
  360.5 62.2 %collective-permute-start.23 = (bf16[2,4096,512]{2,1,0:T(8,128)(2,1)}, bf16[2,4096,512]{2,1,0:T(8,128)(2,1)}, u32[]{:S(2)}, u32[]{:S(2)}) collective-permute-start(bf16[2,4096,512]{2,1,0:T(8,128)(2,1)} %join.1.own_ref), channel_id=1, source_target_pairs={{0,128},{128,0},{1,129},{129,1},{2,130},{130,2},{3,131},{131,3},{4... | collective-permute-start | bytes 25165832 | tf_op jit(solution)/shard_map/ppermute | solution.py:40
  366.8 44.3 %all-to-all-start = ((bf16[256,16,128]{2,1,0:T(8,128)(2,1)}), bf16[256,16,128]{2,1,0:T(8,128)(2,1)S(1)}, u32[]{:S(2)}, u32[]{:S(2)}) async-start(bf16[256,16,128]{2,1,0:T(8,128)(2,1)} %pack.1), calls=%async_computation | async-start | bytes 2097152 | tf_op jit(solution)/shard_map/all_to_all | solution.py:333
  417.9 20.9 %collective-permute-start = (bf16[144,144]{1,0:T(8,128)(2,1)S(1)}, bf16[144,144]{1,0:T(8,128)(2,1)S(1)}, u32[]{:S(2)}, u32[]{:S(2)}) collective-permute-start(bf16[144,144]{1,0:T(8,128)(2,1)S(1)} %reshape.21), channel_id=1, source_target_pairs={{0,256},{256,0},{1,257},{257,1},{2,258},{258,2},{3,259},{259,3},{4... | collective-permute-start | bytes 124424 | tf_op jit(solution)/shard_map/ppermute | solution.py:40
  435.9 20.9 %collective-permute-start.25 = (bf16[1,144,1024]{2,1,0:T(8,128)(2,1)S(1)}, bf16[1,144,1024]{2,1,0:T(8,128)(2,1)S(1)}, u32[]{:S(2)}, u32[]{:S(2)}) collective-permute-start(bf16[1,144,1024]{2,1,0:T(8,128)(2,1)S(1)} %get-tuple-element.8.came_ref), channel_id=1, source_target_pairs={{0,256},{256,0},{1,257},{257,1},{2,258},{258,2},{3,259},{259,3},{4... | collective-permute-start | bytes 884744 | tf_op jit(solution)/shard_map/ppermute | solution.py:40
  451.9 20.9 %collective-permute-start.24 = (bf16[1,144,1024]{2,1,0:T(8,128)(2,1)S(1)}, bf16[1,144,1024]{2,1,0:T(8,128)(2,1)S(1)}, u32[]{:S(2)}, u32[]{:S(2)}) collective-permute-start(bf16[1,144,1024]{2,1,0:T(8,128)(2,1)S(1)} %get-tuple-element.9), channel_id=1, source_target_pairs={{0,256},{256,0},{1,257},{257,1},{2,258},{258,2},{3,259},{259,3},{4... | collective-permute-start | bytes 884744 | tf_op jit(solution)/shard_map/ppermute | solution.py:40
  469.7 16.0 %collective-permute-start.26 = (bf16[1,144,144]{2,1,0:T(8,128)(2,1)S(1)}, bf16[1,144,144]{2,1,0:T(8,128)(2,1)S(1)}, u32[]{:S(2)}, u32[]{:S(2)}) collective-permute-start(bf16[1,144,144]{2,1,0:T(8,128)(2,1)S(1)} %get-tuple-element.11), channel_id=1, source_target_pairs={{0,256},{256,0},{1,257},{257,1},{2,258},{258,2},{3,259},{259,3},{4... | collective-permute-start | bytes 124424 | tf_op jit(solution)/shard_map/ppermute | solution.py:40
  489.8 36.0 %all-to-all-start.1 = ((bf16[256,16,128]{2,1,0:T(8,128)(2,1)}), bf16[256,16,128]{2,1,0:T(8,128)(2,1)S(1)}, u32[]{:S(2)}, u32[]{:S(2)}) async-start(bf16[256,16,128]{2,1,0:T(8,128)(2,1)} %unpick.1), calls=%async_computation.1 | async-start | bytes 2097152 | tf_op jit(solution)/shard_map/all_to_all | solution.py:366
  496.5 8.4 %collective-permute-start.27 = (bf16[1,144,144]{2,1,0:T(8,128)(2,1)S(1)}, bf16[1,144,144]{2,1,0:T(8,128)(2,1)S(1)}, u32[]{:S(2)}, u32[]{:S(2)}) collective-permute-start(bf16[1,144,144]{2,1,0:T(8,128)(2,1)S(1)} %get-tuple-element.13), channel_id=1, source_target_pairs={{0,256},{256,0},{1,257},{257,1},{2,258},{258,2},{3,259},{259,3},{4... | collective-permute-start | bytes 124424 | tf_op jit(solution)/shard_map/ppermute | solution.py:40
  (21 other events, 1899.0 us)

commit v2 on v1

--- a/solution.py
+++ b/solution.py
@@ -116,8 +116,8 @@
 
 
 def join_kernel(pos, *refs):
-    out, sem = refs[-2], refs[-1]
-    pieces = refs[:-2]
+    out_ref, out, sem = refs[-3:]
+    pieces = refs[:-3]
     half = len(pieces) // 2
     z, y = pos[1], pos[2]
 
@@ -140,10 +140,13 @@
         c.start()
     for c in every:
         c.wait()
-
-
-def gather_section(weight, pos):
-    mine = weight[0].T
+    back = pltpu.make_async_copy(out, out_ref, sem)
+    back.start()
+    back.wait()
+
+
+def gather_section(weight, pos, message, arrived):
+    mine, _ = lax.optimization_barrier((weight[0].T, message))
     pair = lax.all_gather(mine, "xl", axis=0, tiled=True)
     a, b = pair[:, :512], pair[:, 512:]
     for bit in DOUBLING:
@@ -154,6 +157,8 @@
     got = [[] for _ in chains]
     held = [c[0] for c in chains]
     for step in range(4):
+        if step == 3:
+            *held, arrived = lax.optimization_barrier((*held, arrived))
         for n, (_, axis, by) in enumerate(chains):
             value = held[n]
             if step == 3:
@@ -167,9 +172,10 @@
         out_shape=jax.ShapeDtypeStruct((2, 4096, 512), BF),
         in_specs=[SMEM] + [ANY] * len(pieces),
         out_specs=ANY,
-        scratch_shapes=[pltpu.SemaphoreType.DMA(())],
+        scratch_shapes=[pltpu.VMEM((2, 4096, 512), BF), pltpu.SemaphoreType.DMA(())],
+        compiler_params=pltpu.CompilerParams(vmem_limit_bytes=60 * MIB),
         name="join",
-    )(pos, *pieces)
+    )(pos, *pieces), arrived
 
 
 def matmul_t(left, right):
@@ -305,7 +311,7 @@
             pltpu.VMEM((2, 2, 4096, 512), BF),
             pltpu.SemaphoreType.DMA((2, 4)),
         ],
-        compiler_params=pltpu.CompilerParams(vmem_limit_bytes=48 * MIB),
+        compiler_params=pltpu.CompilerParams(vmem_limit_bytes=30 * MIB),
         name="sections",
     )(pos, bands, table, raw, came, embed, level, gains, head, own, other)
 
@@ -331,11 +337,11 @@
 
     message = small_call(pack_kernel, 2 * lat_count, (window_table,), to_rows(fields[0]), "pack")
     arrived = lax.all_to_all(message, LAT, 0, 0, tiled=True)
+    own, arrived = gather_section(attn_weight, pos, message, arrived)
     raw_rows = small_call(pick_kernel, WIN_ROWS, scalars, arrived, "pick")
     own_raw = from_rows(raw_rows)
     far_raw = swap(own_raw, "xh", 1)
 
-    own = gather_section(attn_weight, pos)
     other = swap(own, "c", 1)
     gains = lax.all_gather(norm_gain, "c", axis=0, tiled=True)
 

time: 536 us -> 311 us (0.58)
  Pallas kernels: 325 us -> 73.6 us
  blocking collectives: 6.95 us -> 18.2 us
  local copies, waits for them, and re-layouts: 11.5 us -> 20.7 us
    pallas_call x1, Pallas kernels: 256 us -> 7.44 us  [gather_section(): pl.pallas_call(join_kernel, out_shape=jax.ShapeDtypeStruct((2, 4096, 512)...]
    all_to_all x1, waiting for transfers between devices: 28.7 us -> 0.01 us  [per_device(): arrived = lax.all_to_all(message, LAT, 0, 0, tiled=True)]
    ppermute x16, waiting for transfers between devices: 9.65 us -> 25.6 us  [ring(): return lax.ppermute(value, axis, [(i, (i + by) % n) for i in range(n)])]
    ppermute x12, waiting for transfers between devices: 5.57 us -> 20.7 us  [swap(): return lax.ppermute(value, axis, [(i, i ^ bit) for i in range(n)])]
    all_gather x1, blocking collectives: 1.8 us -> 13.1 us  [per_device(): gains = lax.all_gather(norm_gain, 'c', axis=0, tiled=True)]
    unnamed x56, local copies, waits for them, and re-layouts: 5.83 us -> 13.2 us
    all_to_all x1, starting transfers between devices: 6.75 us -> 12.6 us  [per_device(): came_back = lax.all_to_all(reply, LAT, 0, 0, tiled=True)]
  transfers between devices with their start and end apart: 30 -> 30, of which waited for: 10 -> 12; matrix products, arithmetic and copies ran while one was open for 1% -> 1% of each run, Pallas kernels for 11% -> 17%
where the time goes in v2:
time: 311 us; the launch traced here: 310 us
  starting transfers between devices  127 us (41%)
  Pallas kernels  73.6 us (24%)
  waiting for transfers between devices  68.2 us (22%)
  local copies, waits for them, and re-layouts  20.7 us (7%)
  blocking collectives  18.2 us (6%)
    ppermute x12, starting transfers between devices, swap(): return lax.ppermute(value, axis, [(i, i ^ bit) for i in range(n)])  54.2 us
    ppermute x16, starting transfers between devices, ring(): return lax.ppermute(value, axis, [(i, (i + by) % n) for i in range(n)])  49.5 us
    pallas_call x4, Pallas kernels, two_sections(): pl.pallas_call(sections_kernel, out_shape=(jax.ShapeDtypeStruct((slabs, W...  49.4 us
    ppermute x16, waiting for transfers between devices, ring(): return lax.ppermute(value, axis, [(i, (i + by) % n) for i in range(n)])  25.6 us
    all_to_all x1, waiting for transfers between devices, per_device(): came_back = lax.all_to_all(reply, LAT, 0, 0, tiled=True)  21.9 us
    ppermute x12, waiting for transfers between devices, swap(): return lax.ppermute(value, axis, [(i, i ^ bit) for i in range(n)])  20.7 us
    pallas_call x4, Pallas kernels, small_call(): pl.pallas_call(body, out_shape=jax.ShapeDtypeStruct((out_rows, PACK, 128)...  16.8 us
    unnamed x56, local copies, waits for them, and re-layouts  13.2 us
  transfers between devices with their start and end apart: 30, of which 12 were waited for; matrix products, arithmetic and copies ran while one was open for 1% of the time, Pallas kernels for 17%

profile of v2, /device:TPU:8, one launch (start us, length us, event | category | flops | bytes accessed | tf_op | source)
XLA Modules:
  0.0 309.7 jit_solution(6586761184476543676)
XLA Ops:
  2.4 3.4 %pack.1 = bf16[256,16,128]{2,1,0:T(8,128)(2,1)} custom-call(s32[128]{0:T(128)} %table.15, bf16[14,16,128]{2,1,0:T(8,128)(2,1)} %slice.36.rows_ref), custom_call_target="tpu_custom_call" | custom-call | tf_op jit(solution)/shard_map/pack/pallas_call | solution.py:320
  5.8 5.1 %all_gather.6 = bf16[64,1024]{1,0:T(8,128)(2,1)S(1)} all-gather(bf16[32,1024]{1,0:T(8,128)(2,1)} %bitcast.40), channel_id=1, replica_groups=mesh['xh'=2,'c'=2,'z'=8,'y'=8,'xl'=2] {'xl'}, dimensions={0}, use_global_device_ids=true | all-gather | bytes 196608 | tf_op jit(solution)/shard_map/all_gather | solution.py:150
  11.0 6.8 %collective-permute-start = (bf16[64,512]{1,0:T(8,128)(2,1)S(1)}, bf16[64,512]{1,0:T(8,128)(2,1)S(1)}, u32[]{:S(2)}, u32[]{:S(2)}) collective-permute-start(bf16[64,512]{1,0:T(8,128)(2,1)S(1)} %get-tuple-element.31), channel_id=1, source_target_pairs={{0,8},{2,10},{4,12},{6,14},{8,0},{10,2},{12,4},{14,6},{1,9},{3,11}... | collective-permute-start | bytes 196616 | tf_op jit(solution)/shard_map/ppermute | solution.py:40
  17.8 10.9 %collective-permute-start.9 = (bf16[64,512]{1,0:T(8,128)(2,1)S(1)}, bf16[64,512]{1,0:T(8,128)(2,1)S(1)}, u32[]{:S(2)}, u32[]{:S(2)}) collective-permute-start(bf16[64,512]{1,0:T(8,128)(2,1)S(1)} %get-tuple-element.30), channel_id=1, source_target_pairs={{0,64},{16,80},{32,96},{48,112},{64,0},{80,16},{96,32},{112,48},{1... | collective-permute-start | bytes 196616 | tf_op jit(solution)/shard_map/ppermute | solution.py:40
  31.5 4.6 %collective-permute-start.10 = (bf16[128,512]{1,0:T(8,128)(2,1)S(1)}, bf16[128,512]{1,0:T(8,128)(2,1)S(1)}, u32[]{:S(2)}, u32[]{:S(2)}) collective-permute-start(bf16[128,512]{1,0:T(8,128)(2,1)S(1)} %pad_maximum_fusion.5), channel_id=1, source_target_pairs={{0,32},{16,48},{32,0},{48,16},{64,96},{80,112},{96,64},{112,80},{1... | collective-permute-start | bytes 393224 | tf_op jit(solution)/shard_map/ppermute | solution.py:40
  36.7 4.6 %collective-permute-start.2 = (bf16[256,512]{1,0:T(8,128)(2,1)S(1)}, bf16[256,512]{1,0:T(8,128)(2,1)S(1)}, u32[]{:S(2)}, u32[]{:S(2)}) collective-permute-start(bf16[256,512]{1,0:T(8,128)(2,1)S(1)} %pad_maximum_fusion.2), channel_id=1, source_target_pairs={{0,2},{2,0},{4,6},{6,4},{8,10},{10,8},{12,14},{14,12},{1,3},{3,1},... | collective-permute-start | bytes 786440 | tf_op jit(solution)/shard_map/ppermute | solution.py:40
  41.2 10.5 %all-to-all-start = ((bf16[256,16,128]{2,1,0:T(8,128)(2,1)}), bf16[256,16,128]{2,1,0:T(8,128)(2,1)S(1)}, u32[]{:S(2)}, u32[]{:S(2)}) async-start(bf16[256,16,128]{2,1,0:T(8,128)(2,1)} %pack.1), calls=%async_computation | async-start | bytes 2097152 | tf_op jit(solution)/shard_map/all_to_all | solution.py:339
  51.8 3.4 %collective-permute-start.11 = (bf16[256,512]{1,0:T(8,128)(2,1)S(1)}, bf16[256,512]{1,0:T(8,128)(2,1)S(1)}, u32[]{:S(2)}, u32[]{:S(2)}) collective-permute-start(bf16[256,512]{1,0:T(8,128)(2,1)S(1)} %pad_maximum_fusion.3), channel_id=1, source_target_pairs={{0,16},{16,0},{32,48},{48,32},{64,80},{80,64},{96,112},{112,96},{1... | collective-permute-start | bytes 786440 | tf_op jit(solution)/shard_map/ppermute | solution.py:40
  55.2 5.1 %collective-permute-start.6 = (bf16[512,512]{1,0:T(8,128)(2,1)S(1)}, bf16[512,512]{1,0:T(8,128)(2,1)S(1)}, u32[]{:S(2)}, u32[]{:S(2)}) collective-permute-start(bf16[512,512]{1,0:T(8,128)(2,1)S(1)} %pad_maximum_fusion.refs_0_), channel_id=1, source_target_pairs={{0,112},{16,0},{32,16},{48,32},{64,48},{80,64},{96,80},{112,96},{1... | collective-permute-start | bytes 1572872 | tf_op jit(solution)/shard_map/ppermute | solution.py:35
  62.3 16.1 %collective-permute-done.11 = bf16[256,512]{1,0:T(8,128)(2,1)S(1)} collective-permute-done((bf16[256,512]{1,0:T(8,128)(2,1)S(1)}, bf16[256,512]{1,0:T(8,128)(2,1)S(1)}, u32[]{:S(2)}, u32[]{:S(2)}) %collective-permute-start.11) | collective-permute-done | bytes 262176 | tf_op jit(solution)/shard_map/ppermute | solution.py:40
  78.4 3.5 %collective-permute-start.15 = (bf16[512,512]{1,0:T(8,128)(2,1)S(1)}, bf16[512,512]{1,0:T(8,128)(2,1)S(1)}, u32[]{:S(2)}, u32[]{:S(2)}) collective-permute-start(bf16[512,512]{1,0:T(8,128)(2,1)S(1)} %pad_maximum_fusion.1.refs_9_), channel_id=1, source_target_pairs={{0,14},{2,0},{4,2},{6,4},{8,6},{10,8},{12,10},{14,12},{1,15},{3,1}... | collective-permute-start | bytes 1572872 | tf_op jit(solution)/shard_map/ppermute | solution.py:35
  84.3 4.3 %collective-permute-done.6.refs_4_ = bf16[512,512]{1,0:T(8,128)(2,1)S(1)} collective-permute-done((bf16[512,512]{1,0:T(8,128)(2,1)S(1)}, bf16[512,512]{1,0:T(8,128)(2,1)S(1)}, u32[]{:S(2)}, u32[]{:S(2)}) %collective-permute-start.6) | collective-permute-done | bytes 524320 | tf_op jit(solution)/shard_map/ppermute | solution.py:35
  103.4 3.9 %collective-permute-start.8 = (bf16[512,512]{1,0:T(8,128)(2,1)S(1)}, bf16[512,512]{1,0:T(8,128)(2,1)S(1)}, u32[]{:S(2)}, u32[]{:S(2)}) collective-permute-start(bf16[512,512]{1,0:T(8,128)(2,1)S(1)} %collective-permute-done.7.refs_5_), channel_id=1, source_target_pairs={{0,112},{16,0},{32,16},{48,32},{64,48},{80,64},{96,80},{112,96},{1... | collective-permute-start | bytes 1572872 | tf_op jit(solution)/shard_map/ppermute | solution.py:35
  118.1 4.0 %collective-permute-done.5.refs_3_ = bf16[512,512]{1,0:T(8,128)(2,1)S(1)} collective-permute-done((bf16[512,512]{1,0:T(8,128)(2,1)S(1)}, bf16[512,512]{1,0:T(8,128)(2,1)S(1)}, u32[]{:S(2)}, u32[]{:S(2)}) %collective-permute-start.5) | collective-permute-done | bytes 524320 | tf_op jit(solution)/shard_map/ppermute | solution.py:35
  131.9 4.8 %collective-permute-start.22 = (bf16[256,512]{1,0:T(8,128)(2,1)}, bf16[256,512]{1,0:T(8,128)(2,1)}, u32[]{:S(2)}, u32[]{:S(2)}) collective-permute-start(bf16[256,512]{1,0:T(8,128)(2,1)} %slice.30), channel_id=1, source_target_pairs={{0,14},{2,0},{4,2},{6,4},{8,6},{10,8},{12,10},{14,12},{1,15},{3,1}... | collective-permute-start | bytes 786440 | tf_op jit(solution)/shard_map/ppermute | solution.py:35
  138.7 4.6 %collective-permute-start.20 = (bf16[256,512]{1,0:T(8,128)(2,1)}, bf16[256,512]{1,0:T(8,128)(2,1)}, u32[]{:S(2)}, u32[]{:S(2)}) collective-permute-start(bf16[256,512]{1,0:T(8,128)(2,1)} %slice.28), channel_id=1, source_target_pairs={{0,112},{16,0},{32,16},{48,32},{64,48},{80,64},{96,80},{112,96},{1... | collective-permute-start | bytes 786440 | tf_op jit(solution)/shard_map/ppermute | solution.py:35
  147.5 5.6 %collective-permute-done.19.refs_7_ = bf16[256,512]{1,0:T(8,128)(2,1)} collective-permute-done((bf16[256,512]{1,0:T(8,128)(2,1)}, bf16[256,512]{1,0:T(8,128)(2,1)}, u32[]{:S(2)}, u32[]{:S(2)}) %collective-permute-start.19) | collective-permute-done | bytes 262176 | tf_op jit(solution)/shard_map/ppermute | solution.py:35
  153.1 7.4 %join.1.own_ref = bf16[2,4096,512]{2,1,0:T(8,128)(2,1)} custom-call(s32[5]{0:T(128)} %stack.23.where.pos, bf16[512,512]{1,0:T(8,128)(2,1)} %copy-done.9, bf16[512,512]{1,0:T(8,128)(2,1)} %copy-done.15, bf16[512,512]{1,0:T(8,128)(2,1)} %copy-done.19, bf16[512,512]{1,0:T(8,128)(2,1)} %copy-done.12, bf16[512,512]{1,0:T(8,128)(2,1)} %copy-done.14, ...), custom_call_target="tpu_custom_call" | custom-call | tf_op jit(solution)/shard_map/join/pallas_call | solution.py:170
  162.5 13.1 %all-gather = f32[2,1,1024]{2,1,0:T(1,128)S(1)} all-gather(f32[1,1,1024]{2,1,0:T(1,128)S(1)} %bitcast.41), channel_id=1, replica_groups=mesh['xh'=2,'c'=2,'z'=8,'y'=8,'xl'=2] {'c'}, dimensions={0}, use_global_device_ids=true | all-gather | bytes 12288 | tf_op jit(solution)/shard_map/all_gather | solution.py:346
  176.8 4.7 %pick.1 = bf16[12,16,128]{2,1,0:T(8,128)(2,1)} custom-call(s32[5]{0:T(128)} %stack.23.where.pos, s32[128]{0:T(128)} %bands.13, s32[128]{0:T(128)} %table.15, bf16[256,16,128]{2,1,0:T(8,128)(2,1)} %copy-done.7), custom_call_target="tpu_custom_call" | custom-call | tf_op jit(solution)/shard_map/pick/pallas_call | solution.py:320
  182.6 4.6 %collective-permute-start.18 = (bf16[144,144]{1,0:T(8,128)(2,1)S(1)}, bf16[144,144]{1,0:T(8,128)(2,1)S(1)}, u32[]{:S(2)}, u32[]{:S(2)}) collective-permute-start(bf16[144,144]{1,0:T(8,128)(2,1)S(1)} %reshape.21), channel_id=1, source_target_pairs={{0,256},{256,0},{1,257},{257,1},{2,258},{258,2},{3,259},{259,3},{4... | collective-permute-start | bytes 124424 | tf_op jit(solution)/shard_map/ppermute | solution.py:40
  190.7 12.3 %sections.4 = (bf16[1,144,1024]{2,1,0:T(8,128)(2,1)S(1)}, bf16[1,144,144]{2,1,0:T(8,128)(2,1)}, bf16[1,144,144]{2,1,0:T(8,128)(2,1)}) custom-call(s32[5]{0:T(128)S(1)} %copy-done.4, s32[128]{0:T(128)S(1)} %copy-done.6, s32[128]{0:T(128)S(1)} %copy-done.5, bf16[1,144,144]{2,1,0:T(8,128)(2,1)S(1)} %broadcast_in_dim_reshape.6.raw_ref, ...), custom_call_target="tpu_custom_call" | custom-call | tf_op jit(solution)/shard_map/sections/pallas_call | solution.py:301
  205.7 12.4 %sections.5 = (bf16[1,144,1024]{2,1,0:T(8,128)(2,1)S(1)}, bf16[1,144,144]{2,1,0:T(8,128)(2,1)}, bf16[1,144,144]{2,1,0:T(8,128)(2,1)}) custom-call(s32[5]{0:T(128)S(1)} %copy-done.4, s32[128]{0:T(128)S(1)} %copy-done.6, s32[128]{0:T(128)S(1)} %copy-done.5, bf16[1,144,144]{2,1,0:T(8,128)(2,1)S(1)} %bitcast.25, ...), custom_call_target="tpu_custom_call" | custom-call | tf_op jit(solution)/shard_map/sections/pallas_call | solution.py:301
  218.1 4.6 %collective-permute-start.24 = (bf16[1,144,1024]{2,1,0:T(8,128)(2,1)S(1)}, bf16[1,144,1024]{2,1,0:T(8,128)(2,1)S(1)}, u32[]{:S(2)}, u32[]{:S(2)}) collective-permute-start(bf16[1,144,1024]{2,1,0:T(8,128)(2,1)S(1)} %get-tuple-element.21), channel_id=1, source_target_pairs={{0,256},{256,0},{1,257},{257,1},{2,258},{258,2},{3,259},{259,3},{4... | collective-permute-start | bytes 884744 | tf_op jit(solution)/shard_map/ppermute | solution.py:40
  222.8 12.3 %sections.7 = (bf16[1,144,1024]{2,1,0:T(8,128)(2,1)}, bf16[1,144,144]{2,1,0:T(8,128)(2,1)S(1)}, bf16[1,144,144]{2,1,0:T(8,128)(2,1)S(1)}) custom-call(s32[5]{0:T(128)S(1)} %copy-done.4, s32[128]{0:T(128)S(1)} %copy-done.6, s32[128]{0:T(128)S(1)} %copy-done.5, bf16[1,144,144]{2,1,0:T(8,128)(2,1)S(1)} %bitcast.26, ...), custom_call_target="tpu_custom_call" | custom-call | tf_op jit(solution)/shard_map/sections/pallas_call | solution.py:301
  237.8 3.4 %copy-done.1 = bf16[2,4096,512]{2,1,0:T(8,128)(2,1)S(1)} copy-done((bf16[2,4096,512]{2,1,0:T(8,128)(2,1)S(1)}, bf16[2,4096,512]{2,1,0:T(8,128)(2,1)}, u32[]{:S(2)}) %copy-start.1) | copy-done | bytes 8388632
  241.2 12.4 %sections.6 = (bf16[1,144,1024]{2,1,0:T(8,128)(2,1)}, bf16[1,144,144]{2,1,0:T(8,128)(2,1)S(1)}, bf16[1,144,144]{2,1,0:T(8,128)(2,1)S(1)}) custom-call(s32[5]{0:T(128)S(1)} %copy-done.4, s32[128]{0:T(128)S(1)} %copy-done.6, s32[128]{0:T(128)S(1)} %copy-done.5, bf16[1,144,144]{2,1,0:T(8,128)(2,1)S(1)} %bitcast.27, ...), custom_call_target="tpu_custom_call" | custom-call | tf_op jit(solution)/shard_map/sections/pallas_call | solution.py:301
  257.6 12.6 %all-to-all-start.1 = ((bf16[256,16,128]{2,1,0:T(8,128)(2,1)}), bf16[256,16,128]{2,1,0:T(8,128)(2,1)S(1)}, u32[]{:S(2)}, u32[]{:S(2)}) async-start(bf16[256,16,128]{2,1,0:T(8,128)(2,1)} %unpick.1), calls=%async_computation.1 | async-start | bytes 2097152 | tf_op jit(solution)/shard_map/all_to_all | solution.py:372
  270.2 4.6 %collective-permute-start.27 = (bf16[1,144,144]{2,1,0:T(8,128)(2,1)S(1)}, bf16[1,144,144]{2,1,0:T(8,128)(2,1)S(1)}, u32[]{:S(2)}, u32[]{:S(2)}) collective-permute-start(bf16[1,144,144]{2,1,0:T(8,128)(2,1)S(1)} %get-tuple-element.25), channel_id=1, source_target_pairs={{0,256},{256,0},{1,257},{257,1},{2,258},{258,2},{3,259},{259,3},{4... | collective-permute-start | bytes 124424 | tf_op jit(solution)/shard_map/ppermute | solution.py:40
  274.9 4.0 %collective-permute-done.27 = bf16[1,144,144]{2,1,0:T(8,128)(2,1)S(1)} collective-permute-done((bf16[1,144,144]{2,1,0:T(8,128)(2,1)S(1)}, bf16[1,144,144]{2,1,0:T(8,128)(2,1)S(1)}, u32[]{:S(2)}, u32[]{:S(2)}) %collective-permute-start.27) | collective-permute-done | bytes 41504 | tf_op jit(solution)/shard_map/ppermute | solution.py:40
  279.5 21.9 %all-to-all-done.1.came_ref = bf16[256,16,128]{2,1,0:T(8,128)(2,1)S(1)} async-done(((bf16[256,16,128]{2,1,0:T(8,128)(2,1)}), bf16[256,16,128]{2,1,0:T(8,128)(2,1)S(1)}, u32[]{:S(2)}, u32[]{:S(2)}) %all-to-all-start.1) | async-done | bytes 1048608 | tf_op jit(solution)/shard_map/all_to_all | solution.py:372
  302.5 5.5 %unpack.1 = bf16[14,16,128]{2,1,0:T(8,128)(2,1)} custom-call(s32[5]{0:T(128)} %stack.23.where.pos, s32[128]{0:T(128)} %bands.13, s32[128]{0:T(128)} %table.15, bf16[256,16,128]{2,1,0:T(8,128)(2,1)} %copy-done.8), custom_call_target="tpu_custom_call" | custom-call | tf_op jit(solution)/shard_map/unpack/pallas_call | solution.py:320
  (121 shorter events, 71.1 us)
Async XLA Ops:
  11.0 17.8 %collective-permute-start = (bf16[64,512]{1,0:T(8,128)(2,1)S(1)}, bf16[64,512]{1,0:T(8,128)(2,1)S(1)}, u32[]{:S(2)}, u32[]{:S(2)}) collective-permute-start(bf16[64,512]{1,0:T(8,128)(2,1)S(1)} %get-tuple-element.31), channel_id=1, source_target_pairs={{0,8},{2,10},{4,12},{6,14},{8,0},{10,2},{12,4},{14,6},{1,9},{3,11}... | collective-permute-start | bytes 196616 | tf_op jit(solution)/shard_map/ppermute | solution.py:40
  17.8 13.7 %collective-permute-start.9 = (bf16[64,512]{1,0:T(8,128)(2,1)S(1)}, bf16[64,512]{1,0:T(8,128)(2,1)S(1)}, u32[]{:S(2)}, u32[]{:S(2)}) collective-permute-start(bf16[64,512]{1,0:T(8,128)(2,1)S(1)} %get-tuple-element.30), channel_id=1, source_target_pairs={{0,64},{16,80},{32,96},{48,112},{64,0},{80,16},{96,32},{112,48},{1... | collective-permute-start | bytes 196616 | tf_op jit(solution)/shard_map/ppermute | solution.py:40
  28.8 7.9 %collective-permute-start.1 = (bf16[128,512]{1,0:T(8,128)(2,1)S(1)}, bf16[128,512]{1,0:T(8,128)(2,1)S(1)}, u32[]{:S(2)}, u32[]{:S(2)}) collective-permute-start(bf16[128,512]{1,0:T(8,128)(2,1)S(1)} %pad_maximum_fusion.4), channel_id=1, source_target_pairs={{0,4},{2,6},{4,0},{6,2},{8,12},{10,14},{12,8},{14,10},{1,5},{3,7},... | collective-permute-start | bytes 393224 | tf_op jit(solution)/shard_map/ppermute | solution.py:40
  31.5 20.2 %collective-permute-start.10 = (bf16[128,512]{1,0:T(8,128)(2,1)S(1)}, bf16[128,512]{1,0:T(8,128)(2,1)S(1)}, u32[]{:S(2)}, u32[]{:S(2)}) collective-permute-start(bf16[128,512]{1,0:T(8,128)(2,1)S(1)} %pad_maximum_fusion.5), channel_id=1, source_target_pairs={{0,32},{16,48},{32,0},{48,16},{64,96},{80,112},{96,64},{112,80},{1... | collective-permute-start | bytes 393224 | tf_op jit(solution)/shard_map/ppermute | solution.py:40
  36.7 18.5 %collective-permute-start.2 = (bf16[256,512]{1,0:T(8,128)(2,1)S(1)}, bf16[256,512]{1,0:T(8,128)(2,1)S(1)}, u32[]{:S(2)}, u32[]{:S(2)}) collective-permute-start(bf16[256,512]{1,0:T(8,128)(2,1)S(1)} %pad_maximum_fusion.2), channel_id=1, source_target_pairs={{0,2},{2,0},{4,6},{6,4},{8,10},{10,8},{12,14},{14,12},{1,3},{3,1},... | collective-permute-start | bytes 786440 | tf_op jit(solution)/shard_map/ppermute | solution.py:40
  41.2 85.8 %all-to-all-start = ((bf16[256,16,128]{2,1,0:T(8,128)(2,1)}), bf16[256,16,128]{2,1,0:T(8,128)(2,1)S(1)}, u32[]{:S(2)}, u32[]{:S(2)}) async-start(bf16[256,16,128]{2,1,0:T(8,128)(2,1)} %pack.1), calls=%async_computation | async-start | bytes 2097152 | tf_op jit(solution)/shard_map/all_to_all | solution.py:339
  51.8 26.6 %collective-permute-start.11 = (bf16[256,512]{1,0:T(8,128)(2,1)S(1)}, bf16[256,512]{1,0:T(8,128)(2,1)S(1)}, u32[]{:S(2)}, u32[]{:S(2)}) collective-permute-start(bf16[256,512]{1,0:T(8,128)(2,1)S(1)} %pad_maximum_fusion.3), channel_id=1, source_target_pairs={{0,16},{16,0},{32,48},{48,32},{64,80},{80,64},{96,112},{112,96},{1... | collective-permute-start | bytes 786440 | tf_op jit(solution)/shard_map/ppermute | solution.py:40
  55.2 97.9 %copy-start.9 = (bf16[512,512]{1,0:T(8,128)(2,1)}, bf16[512,512]{1,0:T(8,128)(2,1)S(1)}, u32[]{:S(2)}) copy-start(bf16[512,512]{1,0:T(8,128)(2,1)S(1)} %pad_maximum_fusion.refs_0_) | copy-start | bytes 1572868
  55.2 33.4 %collective-permute-start.6 = (bf16[512,512]{1,0:T(8,128)(2,1)S(1)}, bf16[512,512]{1,0:T(8,128)(2,1)S(1)}, u32[]{:S(2)}, u32[]{:S(2)}) collective-permute-start(bf16[512,512]{1,0:T(8,128)(2,1)S(1)} %pad_maximum_fusion.refs_0_), channel_id=1, source_target_pairs={{0,112},{16,0},{32,16},{48,32},{64,48},{80,64},{96,80},{112,96},{1... | collective-permute-start | bytes 1572872 | tf_op jit(solution)/shard_map/ppermute | solution.py:35
  60.4 31.0 %collective-permute-start.3 = (bf16[512,512]{1,0:T(8,128)(2,1)S(1)}, bf16[512,512]{1,0:T(8,128)(2,1)S(1)}, u32[]{:S(2)}, u32[]{:S(2)}) collective-permute-start(bf16[512,512]{1,0:T(8,128)(2,1)S(1)} %pad_maximum_fusion.refs_0_), channel_id=1, source_target_pairs={{0,16},{16,32},{32,48},{48,64},{64,80},{80,96},{96,112},{112,0},{1... | collective-permute-start | bytes 1572872 | tf_op jit(solution)/shard_map/ppermute | solution.py:35
  78.4 74.7 %copy-start.10 = (bf16[512,512]{1,0:T(8,128)(2,1)}, bf16[512,512]{1,0:T(8,128)(2,1)S(1)}, u32[]{:S(2)}) copy-start(bf16[512,512]{1,0:T(8,128)(2,1)S(1)} %pad_maximum_fusion.1.refs_9_) | copy-start | bytes 1572868
  78.4 16.1 %collective-permute-start.15 = (bf16[512,512]{1,0:T(8,128)(2,1)S(1)}, bf16[512,512]{1,0:T(8,128)(2,1)S(1)}, u32[]{:S(2)}, u32[]{:S(2)}) collective-permute-start(bf16[512,512]{1,0:T(8,128)(2,1)S(1)} %pad_maximum_fusion.1.refs_9_), channel_id=1, source_target_pairs={{0,14},{2,0},{4,2},{6,4},{8,6},{10,8},{12,10},{14,12},{1,15},{3,1}... | collective-permute-start | bytes 1572872 | tf_op jit(solution)/shard_map/ppermute | solution.py:35
  81.9 15.6 %collective-permute-start.12 = (bf16[512,512]{1,0:T(8,128)(2,1)S(1)}, bf16[512,512]{1,0:T(8,128)(2,1)S(1)}, u32[]{:S(2)}, u32[]{:S(2)}) collective-permute-start(bf16[512,512]{1,0:T(8,128)(2,1)S(1)} %pad_maximum_fusion.1.refs_9_), channel_id=1, source_target_pairs={{0,2},{2,4},{4,6},{6,8},{8,10},{10,12},{12,14},{14,0},{1,3},{3,5},... | collective-permute-start | bytes 1572872 | tf_op jit(solution)/shard_map/ppermute | solution.py:35
  88.6 14.8 %collective-permute-start.7 = (bf16[512,512]{1,0:T(8,128)(2,1)S(1)}, bf16[512,512]{1,0:T(8,128)(2,1)S(1)}, u32[]{:S(2)}, u32[]{:S(2)}) collective-permute-start(bf16[512,512]{1,0:T(8,128)(2,1)S(1)} %collective-permute-done.6.refs_4_), channel_id=1, source_target_pairs={{0,112},{16,0},{32,16},{48,32},{64,48},{80,64},{96,80},{112,96},{1... | collective-permute-start | bytes 1572872 | tf_op jit(solution)/shard_map/ppermute | solution.py:35
  91.4 15.9 %collective-permute-start.4 = (bf16[512,512]{1,0:T(8,128)(2,1)S(1)}, bf16[512,512]{1,0:T(8,128)(2,1)S(1)}, u32[]{:S(2)}, u32[]{:S(2)}) collective-permute-start(bf16[512,512]{1,0:T(8,128)(2,1)S(1)} %collective-permute-done.3.refs_1_), channel_id=1, source_target_pairs={{0,16},{16,32},{32,48},{48,64},{64,80},{80,96},{96,112},{112,0},{1... | collective-permute-start | bytes 1572872 | tf_op jit(solution)/shard_map/ppermute | solution.py:35
  94.5 14.8 %collective-permute-start.16 = (bf16[512,512]{1,0:T(8,128)(2,1)S(1)}, bf16[512,512]{1,0:T(8,128)(2,1)S(1)}, u32[]{:S(2)}, u32[]{:S(2)}) collective-permute-start(bf16[512,512]{1,0:T(8,128)(2,1)S(1)} %collective-permute-done.15.refs_13_), channel_id=1, source_target_pairs={{0,14},{2,0},{4,2},{6,4},{8,6},{10,8},{12,10},{14,12},{1,15},{3,1}... | collective-permute-start | bytes 1572872 | tf_op jit(solution)/shard_map/ppermute | solution.py:35
  97.5 15.0 %collective-permute-start.13 = (bf16[512,512]{1,0:T(8,128)(2,1)S(1)}, bf16[512,512]{1,0:T(8,128)(2,1)S(1)}, u32[]{:S(2)}, u32[]{:S(2)}) collective-permute-start(bf16[512,512]{1,0:T(8,128)(2,1)S(1)} %collective-permute-done.12.refs_10_), channel_id=1, source_target_pairs={{0,2},{2,4},{4,6},{6,8},{8,10},{10,12},{12,14},{14,0},{1,3},{3,5},... | collective-permute-start | bytes 1572872 | tf_op jit(solution)/shard_map/ppermute | solution.py:35
  103.4 14.6 %collective-permute-start.8 = (bf16[512,512]{1,0:T(8,128)(2,1)S(1)}, bf16[512,512]{1,0:T(8,128)(2,1)S(1)}, u32[]{:S(2)}, u32[]{:S(2)}) collective-permute-start(bf16[512,512]{1,0:T(8,128)(2,1)S(1)} %collective-permute-done.7.refs_5_), channel_id=1, source_target_pairs={{0,112},{16,0},{32,16},{48,32},{64,48},{80,64},{96,80},{112,96},{1... | collective-permute-start | bytes 1572872 | tf_op jit(solution)/shard_map/ppermute | solution.py:35
  107.3 14.7 %collective-permute-start.5 = (bf16[512,512]{1,0:T(8,128)(2,1)S(1)}, bf16[512,512]{1,0:T(8,128)(2,1)S(1)}, u32[]{:S(2)}, u32[]{:S(2)}) collective-permute-start(bf16[512,512]{1,0:T(8,128)(2,1)S(1)} %collective-permute-done.4.refs_2_), channel_id=1, source_target_pairs={{0,16},{16,32},{32,48},{48,64},{64,80},{80,96},{96,112},{112,0},{1... | collective-permute-start | bytes 1572872 | tf_op jit(solution)/shard_map/ppermute | solution.py:35
  109.3 14.1 %collective-permute-start.17 = (bf16[512,512]{1,0:T(8,128)(2,1)S(1)}, bf16[512,512]{1,0:T(8,128)(2,1)S(1)}, u32[]{:S(2)}, u32[]{:S(2)}) collective-permute-start(bf16[512,512]{1,0:T(8,128)(2,1)S(1)} %collective-permute-done.16.refs_14_), channel_id=1, source_target_pairs={{0,14},{2,0},{4,2},{6,4},{8,6},{10,8},{12,10},{14,12},{1,15},{3,1}... | collective-permute-start | bytes 1572872 | tf_op jit(solution)/shard_map/ppermute | solution.py:35
  112.5 14.5 %collective-permute-start.14 = (bf16[512,512]{1,0:T(8,128)(2,1)S(1)}, bf16[512,512]{1,0:T(8,128)(2,1)}, u32[]{:S(2)}, u32[]{:S(2)}) collective-permute-start(bf16[512,512]{1,0:T(8,128)(2,1)S(1)} %collective-permute-done.13.refs_11_), channel_id=1, source_target_pairs={{0,2},{2,4},{4,6},{6,8},{8,10},{10,12},{12,14},{14,0},{1,3},{3,5},... | collective-permute-start | bytes 1572872 | tf_op jit(solution)/shard_map/ppermute | solution.py:35
  131.9 14.0 %collective-permute-start.22 = (bf16[256,512]{1,0:T(8,128)(2,1)}, bf16[256,512]{1,0:T(8,128)(2,1)}, u32[]{:S(2)}, u32[]{:S(2)}) collective-permute-start(bf16[256,512]{1,0:T(8,128)(2,1)} %slice.30), channel_id=1, source_target_pairs={{0,14},{2,0},{4,2},{6,4},{8,6},{10,8},{12,10},{14,12},{1,15},{3,1}... | collective-permute-start | bytes 786440 | tf_op jit(solution)/shard_map/ppermute | solution.py:35
  136.7 9.1 %collective-permute-start.21 = (bf16[256,512]{1,0:T(8,128)(2,1)}, bf16[256,512]{1,0:T(8,128)(2,1)}, u32[]{:S(2)}, u32[]{:S(2)}) collective-permute-start(bf16[256,512]{1,0:T(8,128)(2,1)} %slice.29), channel_id=1, source_target_pairs={{0,2},{2,4},{4,6},{6,8},{8,10},{10,12},{12,14},{14,0},{1,3},{3,5},... | collective-permute-start | bytes 786440 | tf_op jit(solution)/shard_map/ppermute | solution.py:35
  138.7 8.8 %collective-permute-start.20 = (bf16[256,512]{1,0:T(8,128)(2,1)}, bf16[256,512]{1,0:T(8,128)(2,1)}, u32[]{:S(2)}, u32[]{:S(2)}) collective-permute-start(bf16[256,512]{1,0:T(8,128)(2,1)} %slice.28), channel_id=1, source_target_pairs={{0,112},{16,0},{32,16},{48,32},{64,48},{80,64},{96,80},{112,96},{1... | collective-permute-start | bytes 786440 | tf_op jit(solution)/shard_map/ppermute | solution.py:35
  143.3 9.8 %collective-permute-start.19 = (bf16[256,512]{1,0:T(8,128)(2,1)}, bf16[256,512]{1,0:T(8,128)(2,1)}, u32[]{:S(2)}, u32[]{:S(2)}) collective-permute-start(bf16[256,512]{1,0:T(8,128)(2,1)} %slice.27), channel_id=1, source_target_pairs={{0,16},{16,32},{32,48},{48,64},{64,80},{80,96},{96,112},{112,0},{1... | collective-permute-start | bytes 786440 | tf_op jit(solution)/shard_map/ppermute | solution.py:35
  160.6 26.7 %collective-permute-start.23 = (bf16[2,4096,512]{2,1,0:T(8,128)(2,1)}, bf16[2,4096,512]{2,1,0:T(8,128)(2,1)}, u32[]{:S(2)}, u32[]{:S(2)}) collective-permute-start(bf16[2,4096,512]{2,1,0:T(8,128)(2,1)} %join.1.own_ref), channel_id=1, source_target_pairs={{0,128},{128,0},{1,129},{129,1},{2,130},{130,2},{3,131},{131,3},{4... | collective-permute-start | bytes 25165832 | tf_op jit(solution)/shard_map/ppermute | solution.py:40
  182.6 23.2 %collective-permute-start.18 = (bf16[144,144]{1,0:T(8,128)(2,1)S(1)}, bf16[144,144]{1,0:T(8,128)(2,1)S(1)}, u32[]{:S(2)}, u32[]{:S(2)}) collective-permute-start(bf16[144,144]{1,0:T(8,128)(2,1)S(1)} %reshape.21), channel_id=1, source_target_pairs={{0,256},{256,0},{1,257},{257,1},{2,258},{258,2},{3,259},{259,3},{4... | collective-permute-start | bytes 124424 | tf_op jit(solution)/shard_map/ppermute | solution.py:40
  203.0 19.8 %collective-permute-start.25 = (bf16[1,144,1024]{2,1,0:T(8,128)(2,1)S(1)}, bf16[1,144,1024]{2,1,0:T(8,128)(2,1)S(1)}, u32[]{:S(2)}, u32[]{:S(2)}) collective-permute-start(bf16[1,144,1024]{2,1,0:T(8,128)(2,1)S(1)} %get-tuple-element.20.came_ref), channel_id=1, source_target_pairs={{0,256},{256,0},{1,257},{257,1},{2,258},{258,2},{3,259},{259,3},{4... | collective-permute-start | bytes 884744 | tf_op jit(solution)/shard_map/ppermute | solution.py:40
  218.1 19.7 %collective-permute-start.24 = (bf16[1,144,1024]{2,1,0:T(8,128)(2,1)S(1)}, bf16[1,144,1024]{2,1,0:T(8,128)(2,1)S(1)}, u32[]{:S(2)}, u32[]{:S(2)}) collective-permute-start(bf16[1,144,1024]{2,1,0:T(8,128)(2,1)S(1)} %get-tuple-element.21), channel_id=1, source_target_pairs={{0,256},{256,0},{1,257},{257,1},{2,258},{258,2},{3,259},{259,3},{4... | collective-permute-start | bytes 884744 | tf_op jit(solution)/shard_map/ppermute | solution.py:40
  235.1 18.5 %collective-permute-start.26 = (bf16[1,144,144]{2,1,0:T(8,128)(2,1)S(1)}, bf16[1,144,144]{2,1,0:T(8,128)(2,1)S(1)}, u32[]{:S(2)}, u32[]{:S(2)}) collective-permute-start(bf16[1,144,144]{2,1,0:T(8,128)(2,1)S(1)} %get-tuple-element.23), channel_id=1, source_target_pairs={{0,256},{256,0},{1,257},{257,1},{2,258},{258,2},{3,259},{259,3},{4... | collective-permute-start | bytes 124424 | tf_op jit(solution)/shard_map/ppermute | solution.py:40
  257.6 43.8 %all-to-all-start.1 = ((bf16[256,16,128]{2,1,0:T(8,128)(2,1)}), bf16[256,16,128]{2,1,0:T(8,128)(2,1)S(1)}, u32[]{:S(2)}, u32[]{:S(2)}) async-start(bf16[256,16,128]{2,1,0:T(8,128)(2,1)} %unpick.1), calls=%async_computation.1 | async-start | bytes 2097152 | tf_op jit(solution)/shard_map/all_to_all | solution.py:372
  270.2 8.7 %collective-permute-start.27 = (bf16[1,144,144]{2,1,0:T(8,128)(2,1)S(1)}, bf16[1,144,144]{2,1,0:T(8,128)(2,1)S(1)}, u32[]{:S(2)}, u32[]{:S(2)}) collective-permute-start(bf16[1,144,144]{2,1,0:T(8,128)(2,1)S(1)} %get-tuple-element.25), channel_id=1, source_target_pairs={{0,256},{256,0},{1,257},{257,1},{2,258},{258,2},{3,259},{259,3},{4... | collective-permute-start | bytes 124424 | tf_op jit(solution)/shard_map/ppermute | solution.py:40
  (21 other events, 500.8 us)
